TPU v7x, 512 devices: a whole 4x8x8 slice. The times are simulated.
512 devices in a mesh: grp: 64 (over y, x, core), sub: 8 (over z).
Axes of the slice: x: 4, y: 8, z: 8, core: 2. Of those that a mesh axis runs over, the one named last changes fastest.
Arguments:
- velocity: float32 [3, 8192, 4096], P(None, ('grp', 'sub')), may hold values from -6 to 6
- forcing: float32 [3, 8192, 4096], P(None, ('grp', 'sub')), may hold values from -6 to 6
- viscosity: float32 [8192, 4096], P(('grp', 'sub')), may hold values from 0.2 to 2
- coarse_visc: float32 [4096, 1024], P(('grp', 'sub')), may hold values from 0.5 to 5
Outputs:
- corrected: float32 [3, 8192, 4096], P(None, ('grp', 'sub'))
- coarse_fix: float32 [3, 4096, 1024], P(None, ('grp', 'sub'))
All inputs are finite; a program needn't handle non-finite values.
Results may differ from a plain program's by a relative error of at most 0.00002.
Values sent between devices are 32-bit elements; how exact they have to be, the bound alone decides.
No kernel may reach another device: no remote copies, remote signals or barrier semaphores. Data moves between devices by JAX's collectives and lax.ppermute only.
A program may use at most 128 MiB of HBM per device.

v0:
```python
import jax
import jax.numpy as jnp
from jax import lax
from jax.sharding import PartitionSpec as P

NY = 32
NZ = 32
DEGREE = 3


LOWER_EIG = 0.15
UPPER_EIG = 1.95
CENTER = 0.5 * (UPPER_EIG + LOWER_EIG)
HALF_WIDTH = 0.5 * (UPPER_EIG - LOWER_EIG)


def extended_2(block, sides, width):
    for axis, dim in sides:
        count = lax.axis_size(axis)
        forward = [(i, i + 1) for i in range(count - 1)]
        backward = [(target, source) for source, target in forward]
        low = lax.ppermute(
            lax.slice_in_dim(block, block.shape[dim] - width, None, axis=dim), axis, forward
        )
        high = lax.ppermute(lax.slice_in_dim(block, 0, width, axis=dim), axis, backward)
        block = jnp.concatenate([low, block, high], axis=dim)
    return block


def passed_along(block, axis, distance):
    devices = range(lax.axis_size(axis))
    route = [(i - distance, i) for i in devices if i - distance in devices]
    return lax.ppermute(block, axis, route)


def apply_visc(padded, coeff, rows, cols):
    planes = padded.shape[1] - 2
    blocks = padded.reshape(3, planes + 2, rows, cols)
    center = blocks[:, 1:-1]
    beside = blocks[:, 2:] + blocks[:, :-2]
    beside = beside + jnp.roll(center, 1, 2) + jnp.roll(center, -1, 2)
    beside = beside + jnp.roll(center, 1, 3) + jnp.roll(center, -1, 3)
    scaled = coeff.reshape(1, planes, rows, cols)
    return ((1.0 + 6.0 * scaled) * center - scaled * beside).reshape(3, planes, rows * cols)


def restrict_cross(field, rows, cols):
    planes = field.shape[1]
    blocks = field.reshape(3, planes, rows, cols)
    odd_rows = blocks[:, :, 1::2]
    blocks = blocks[:, :, 0::2] + 0.5 * (odd_rows + jnp.roll(odd_rows, 1, 2))
    odd_cols = blocks[:, :, :, 1::2]
    blocks = blocks[:, :, :, 0::2] + 0.5 * (odd_cols + jnp.roll(odd_cols, 1, 3))
    return blocks.reshape(3, planes, rows // 2 * (cols // 2))


def restrict_planes(field, before):
    even_planes = field[:, 0::2]
    odd_planes = field[:, 1::2]
    left_planes = jnp.concatenate([before, odd_planes[:, :-1]], axis=1)
    return 0.125 * (even_planes + 0.5 * (odd_planes + left_planes))


def chebyshev(source, coeff, apply_fn, degree):
    diagonal = 1.0 + 6.0 * coeff[None]
    sigma_ratio = CENTER / HALF_WIDTH
    ratio_old = 1.0 / sigma_ratio
    update = source / (diagonal * CENTER)
    approx = update
    for sweep in range(degree - 1):
        defect = source - apply_fn(approx)
        ratio_new = 1.0 / (2.0 * sigma_ratio - ratio_old)
        update = ratio_new * ratio_old * update + 2.0 * ratio_new / HALF_WIDTH * (defect / diagonal)
        approx = approx + update
        ratio_old = ratio_new
    return approx


def prolong(extended, rows, cols):
    own_planes = extended[:, :-1]
    mid_planes = 0.5 * (own_planes + extended[:, 1:])
    planes = own_planes.shape[1]
    refined = jnp.stack([own_planes, mid_planes], axis=2).reshape(3, 2 * planes, rows, cols)
    mid_rows = 0.5 * (refined + jnp.roll(refined, -1, 2))
    refined = jnp.stack([refined, mid_rows], axis=3).reshape(3, 2 * planes, 2 * rows, cols)
    mid_cols = 0.5 * (refined + jnp.roll(refined, -1, 3))
    refined = jnp.stack([refined, mid_cols], axis=4).reshape(3, 2 * planes, 2 * rows, 2 * cols)
    return refined.reshape(3, 2 * planes, 4 * rows * cols)


def shards(velocity, forcing, viscosity, coarse_visc):
    padded = extended_2(velocity, ((("grp", "sub"), 1),), 1)
    residual = forcing - apply_visc(padded, viscosity, 2 * NY, 2 * NZ)
    crossed = restrict_cross(residual, 2 * NY, 2 * NZ)
    before = passed_along(crossed[:, -1:], ("grp", "sub"), 1)
    coarse_src = restrict_planes(crossed, before)

    def spread_apply(approx):
        widened = extended_2(approx, ((("grp", "sub"), 1),), 1)
        return apply_visc(widened, coarse_visc, NY, NZ)

    coarse_fix = chebyshev(coarse_src, coarse_visc, spread_apply, DEGREE)
    after = passed_along(coarse_fix[:, :1], ("grp", "sub"), -1)
    extended = jnp.concatenate([coarse_fix, after], axis=1)
    corrected = velocity + prolong(extended, NY, NZ)
    return (corrected, coarse_fix)


def solution(mesh):
    return jax.shard_map(
        shards,
        mesh=mesh,
        in_specs=(
            P(None, ("grp", "sub"), None),
            P(None, ("grp", "sub"), None),
            P(("grp", "sub"), None),
            P(("grp", "sub"), None),
        ),
        out_specs=(P(None, ("grp", "sub"), None), P(None, ("grp", "sub"), None)),
        check_vma=False,
    )
```

profile of v0, /device:TPU:32, one launch (start us, length us, event | category | flops | bytes accessed | tf_op | source)
XLA Modules:
  0.0 130.0 jit_solution(9590302302303973052)
XLA Ops:
  0.6 1.3 fusion.36
  1.9 4.3 %collective-permute-start = (f32[3,1,4096]{2,1,0:T(1,128)S(1)}, f32[3,1,4096]{2,1,0:T(1,128)S(1)}, u32[]{:S(2)}, u32[]{:S(2)}) collective-permute-start(f32[3,1,4096]{2,1,0:T(1,128)S(1)} %get-tuple-element.14), channel_id=1, source_target_pairs={{0,1},{1,2},{2,3},{3,4},{4,5},{5,6},{6,7},{7,8},{8,9},{9,10},{10,1... | collective-permute-start | bytes 147464 | tf_op jit(solution)/shard_map/ppermute | solution.py:22
  6.2 10.1 %collective-permute-start.1 = (f32[3,1,4096]{2,1,0:T(1,128)S(1)}, f32[3,1,4096]{2,1,0:T(1,128)S(1)}, u32[]{:S(2)}, u32[]{:S(2)}) collective-permute-start(f32[3,1,4096]{2,1,0:T(1,128)S(1)} %get-tuple-element.15), channel_id=1, source_target_pairs={{1,0},{2,1},{3,2},{4,3},{5,4},{6,5},{7,6},{8,7},{9,8},{10,9},{11,1... | collective-permute-start | bytes 147464 | tf_op jit(solution)/shard_map/ppermute | solution.py:25
  16.3 1.1 reshape.144
  21.5 1.5 %fusion.5 = f32[3,16,64,64]{3,2,1,0:T(8,128)S(1)} fusion(f32[3,18,64,64]{3,2,1,0:T(8,128)S(1)} %reshape.145, f32[3,16,63,64]{3,2,1,0:T(8,128)S(1)} %get-tuple-element.11, f32[3,16,1,64]{3,2,1,0:T(1,128)S(1)} %get-tuple-element.13, f32[3,16,1,64]{3,2,1,0:T(1,128)S(1)} %get-tuple-element.12, f32[3,16,63,64]{3,2,1,0:T(8,128)S(1)} %get-tuple-element.10, ...), kind=kLoop, calls=%fused_computation.8 | loop fusion | flops 2359296 | bytes 6815744 | tf_op jit(solution)/shard_map/sub | solution.py:44
  25.9 1.1 slice.232
  27.4 9.8 %slice.237 = f32[3,16,32,32]{3,2,1,0:T(8,128)S(1)} slice(f32[3,16,32,64]{3,2,1,0:T(8,128)S(1)} %fusion.8), slice={[0:3:1], [0:16:1], [0:32:1], [1:64:2]} | slice | bytes 393216 | tf_op jit(solution)/shard_map/slice | solution.py:52
  37.2 9.6 %slice.236 = f32[3,16,32,32]{3,2,1,0:T(8,128)S(1)} slice(f32[3,16,32,64]{3,2,1,0:T(8,128)S(1)} %fusion.8), slice={[0:3:1], [0:16:1], [0:32:1], [0:64:2]} | slice | bytes 393216 | tf_op jit(solution)/shard_map/slice | solution.py:53
  47.8 1.9 %collective-permute-start.2 = (f32[3,1,1024]{2,1,0:T(1,128)S(1)}, f32[3,1,1024]{2,1,0:T(1,128)S(1)}, u32[]{:S(2)}, u32[]{:S(2)}) collective-permute-start(f32[3,1,1024]{2,1,0:T(1,128)S(1)} %slice.291), channel_id=1, source_target_pairs={{0,1},{1,2},{2,3},{3,4},{4,5},{5,6},{6,7},{7,8},{8,9},{9,10},{10,1... | collective-permute-start | bytes 36872 | tf_op jit(solution)/shard_map/ppermute | solution.py:33
  50.0 8.3 %collective-permute-done.2 = f32[3,1,1024]{2,1,0:T(1,128)S(1)} collective-permute-done((f32[3,1,1024]{2,1,0:T(1,128)S(1)}, f32[3,1,1024]{2,1,0:T(1,128)S(1)}, u32[]{:S(2)}, u32[]{:S(2)}) %collective-permute-start.2) | collective-permute-done | bytes 12320 | tf_op jit(solution)/shard_map/ppermute | solution.py:33
  58.4 1.9 %collective-permute-start.3 = (f32[3,1,1024]{2,1,0:T(1,128)S(1)}, f32[3,1,1024]{2,1,0:T(1,128)S(1)}, u32[]{:S(2)}, u32[]{:S(2)}) collective-permute-start(f32[3,1,1024]{2,1,0:T(1,128)S(1)} %get-tuple-element.34), channel_id=1, source_target_pairs={{0,1},{1,2},{2,3},{3,4},{4,5},{5,6},{6,7},{7,8},{8,9},{9,10},{10,1... | collective-permute-start | bytes 36872 | tf_op jit(solution)/shard_map/ppermute | solution.py:22
  60.3 9.1 %collective-permute-start.4 = (f32[3,1,1024]{2,1,0:T(1,128)S(1)}, f32[3,1,1024]{2,1,0:T(1,128)S(1)}, u32[]{:S(2)}, u32[]{:S(2)}) collective-permute-start(f32[3,1,1024]{2,1,0:T(1,128)S(1)} %get-tuple-element.35), channel_id=1, source_target_pairs={{1,0},{2,1},{3,2},{4,3},{5,4},{6,5},{7,6},{8,7},{9,8},{10,9},{11,1... | collective-permute-start | bytes 36872 | tf_op jit(solution)/shard_map/ppermute | solution.py:25
  69.4 1.4 %collective-permute-done.4 = f32[3,1,1024]{2,1,0:T(1,128)S(1)} collective-permute-done((f32[3,1,1024]{2,1,0:T(1,128)S(1)}, f32[3,1,1024]{2,1,0:T(1,128)S(1)}, u32[]{:S(2)}, u32[]{:S(2)}) %collective-permute-start.4) | collective-permute-done | bytes 12320 | tf_op jit(solution)/shard_map/ppermute | solution.py:25
  72.1 1.9 %collective-permute-start.5 = (f32[3,1,1024]{2,1,0:T(1,128)S(1)}, f32[3,1,1024]{2,1,0:T(1,128)S(1)}, u32[]{:S(2)}, u32[]{:S(2)}) collective-permute-start(f32[3,1,1024]{2,1,0:T(1,128)S(1)} %get-tuple-element.32), channel_id=1, source_target_pairs={{0,1},{1,2},{2,3},{3,4},{4,5},{5,6},{6,7},{7,8},{8,9},{9,10},{10,1... | collective-permute-start | bytes 36872 | tf_op jit(solution)/shard_map/ppermute | solution.py:22
  74.0 9.1 %collective-permute-start.6 = (f32[3,1,1024]{2,1,0:T(1,128)S(1)}, f32[3,1,1024]{2,1,0:T(1,128)S(1)}, u32[]{:S(2)}, u32[]{:S(2)}) collective-permute-start(f32[3,1,1024]{2,1,0:T(1,128)S(1)} %get-tuple-element.33), channel_id=1, source_target_pairs={{1,0},{2,1},{3,2},{4,3},{5,4},{6,5},{7,6},{8,7},{9,8},{10,9},{11,1... | collective-permute-start | bytes 36872 | tf_op jit(solution)/shard_map/ppermute | solution.py:25
  83.1 1.4 %collective-permute-done.6 = f32[3,1,1024]{2,1,0:T(1,128)S(1)} collective-permute-done((f32[3,1,1024]{2,1,0:T(1,128)S(1)}, f32[3,1,1024]{2,1,0:T(1,128)S(1)}, u32[]{:S(2)}, u32[]{:S(2)}) %collective-permute-start.6) | collective-permute-done | bytes 12320 | tf_op jit(solution)/shard_map/ppermute | solution.py:25
  85.9 9.2 %collective-permute-start.7 = (f32[3,1,1024]{2,1,0:T(1,128)S(1)}, f32[3,1,1024]{2,1,0:T(1,128)S(1)}, u32[]{:S(2)}, u32[]{:S(2)}) collective-permute-start(f32[3,1,1024]{2,1,0:T(1,128)S(1)} %slice.319), channel_id=1, source_target_pairs={{1,0},{2,1},{3,2},{4,3},{5,4},{6,5},{7,6},{8,7},{9,8},{10,9},{11,1... | collective-permute-start | bytes 36872 | tf_op jit(solution)/shard_map/ppermute | solution.py:33
  95.1 4.0 %copy.17 = f32[3,16,4096]{1,2,0:T(8,128)} copy(f32[3,16,4096]{2,1,0:T(8,128)S(1)} %copy-done.3) | data formatting | bytes 1572864 | tf_op args[0]
  102.7 1.8 %copy.15 = f32[3,16,64,1,1]{3,1,2,0,4:T(8,128)} copy(f32[3,16,64,1,1]{2,1,0,4,3:T(8,128)S(1)} %bitcast.36) | data formatting | bytes 24576 | tf_op jit(solution)/shard_map/jit(_roll_static)/concatenate | solution.py:86
  104.5 1.9 %fusion.6 = f32[3,16,64,32,1]{3,1,2,0,4:T(8,128)S(1)} fusion(f32[3,16,64,32,1]{3,1,2,0,4:T(8,128)S(1)} %bitcast.29, f32[3,16,64,1,1]{3,1,2,0,4:T(8,128)} %copy.15, f32[3,16,64,31,1]{3,1,2,0,4:T(8,128)S(1)} %slice_bitcast_fusion), kind=kLoop, calls=%fused_computation.12 | loop fusion | flops 294912 | bytes 1179648 | tf_op jit(solution)/shard_map/mul | solution.py:86
  106.4 1.9 %pad_maximum_fusion = f32[3,16,64,32,2]{3,1,2,0,4:T(8,128)} fusion(f32[3,16,64,32,1]{3,1,2,0,4:T(8,128)S(1)} %fusion.6, f32[3,16,64,32,1]{3,1,2,0,4:T(8,128)S(1)} %bitcast.30), kind=kLoop, calls=%fused_computation | loop fusion | flops 196608 | bytes 1572864 | tf_op jit(solution)/shard_map/stack | solution.py:87
  108.4 8.5 %copy.16 = f32[3,16,64,32,2]{1,4,3,2,0:T(2,128)} copy(f32[3,16,64,32,2]{3,1,2,0,4:T(8,128)} %pad_maximum_fusion) | data formatting | bytes 1572864 | tf_op jit(solution)/shard_map/stack | solution.py:87
  116.9 7.9 %add.161 = f32[3,16,4096]{1,2,0:T(8,128)} add(f32[3,16,4096]{1,2,0:T(8,128)} %copy.17, f32[3,16,4096]{1,2,0:T(8,128)} %bitcast.31) | non-fusion elementwise | flops 196608 | bytes 2359296 | tf_op jit(solution)/shard_map/add | solution.py:105
  124.8 5.2 %copy.18 = f32[3,16,4096]{2,1,0:T(8,128)} copy(f32[3,16,4096]{1,2,0:T(8,128)} %add.161) | data formatting | bytes 1572864
  (77 shorter events, 14.6 us)
Async XLA Ops:
  0.6 17.8 %copy-start.2 = (f32[3,16,4096]{2,1,0:T(8,128)S(1)}, f32[3,16,4096]{2,1,0:T(8,128)}, u32[]{:S(2)}) copy-start(f32[3,16,4096]{2,1,0:T(8,128)} %param.4) | copy-start | bytes 2359300
  1.9 16.5 %collective-permute-start = (f32[3,1,4096]{2,1,0:T(1,128)S(1)}, f32[3,1,4096]{2,1,0:T(1,128)S(1)}, u32[]{:S(2)}, u32[]{:S(2)}) collective-permute-start(f32[3,1,4096]{2,1,0:T(1,128)S(1)} %get-tuple-element.14), channel_id=1, source_target_pairs={{0,1},{1,2},{2,3},{3,4},{4,5},{5,6},{6,7},{7,8},{8,9},{9,10},{10,1... | collective-permute-start | bytes 147464 | tf_op jit(solution)/shard_map/ppermute | solution.py:22
  6.2 12.2 %collective-permute-start.1 = (f32[3,1,4096]{2,1,0:T(1,128)S(1)}, f32[3,1,4096]{2,1,0:T(1,128)S(1)}, u32[]{:S(2)}, u32[]{:S(2)}) collective-permute-start(f32[3,1,4096]{2,1,0:T(1,128)S(1)} %get-tuple-element.15), channel_id=1, source_target_pairs={{1,0},{2,1},{3,2},{4,3},{5,4},{6,5},{7,6},{8,7},{9,8},{10,9},{11,1... | collective-permute-start | bytes 147464 | tf_op jit(solution)/shard_map/ppermute | solution.py:25
  17.5 1.0 copy-start
  20.3 1.0 copy-start.1
  20.3 1.2 copy-start.4
  22.9 1.1 copy-start.6
  47.1 2.7 %copy-start.7 = (f32[8,1024]{1,0:T(8,128)S(1)}, f32[8,1024]{1,0:T(8,128)}, u32[]{:S(2)}) copy-start(f32[8,1024]{1,0:T(8,128)} %param.7) | copy-start | bytes 98308
  47.8 10.4 %collective-permute-start.2 = (f32[3,1,1024]{2,1,0:T(1,128)S(1)}, f32[3,1,1024]{2,1,0:T(1,128)S(1)}, u32[]{:S(2)}, u32[]{:S(2)}) collective-permute-start(f32[3,1,1024]{2,1,0:T(1,128)S(1)} %slice.291), channel_id=1, source_target_pairs={{0,1},{1,2},{2,3},{3,4},{4,5},{5,6},{6,7},{7,8},{8,9},{9,10},{10,1... | collective-permute-start | bytes 36872 | tf_op jit(solution)/shard_map/ppermute | solution.py:33
  58.4 11.0 %collective-permute-start.3 = (f32[3,1,1024]{2,1,0:T(1,128)S(1)}, f32[3,1,1024]{2,1,0:T(1,128)S(1)}, u32[]{:S(2)}, u32[]{:S(2)}) collective-permute-start(f32[3,1,1024]{2,1,0:T(1,128)S(1)} %get-tuple-element.34), channel_id=1, source_target_pairs={{0,1},{1,2},{2,3},{3,4},{4,5},{5,6},{6,7},{7,8},{8,9},{9,10},{10,1... | collective-permute-start | bytes 36872 | tf_op jit(solution)/shard_map/ppermute | solution.py:22
  60.3 10.5 %collective-permute-start.4 = (f32[3,1,1024]{2,1,0:T(1,128)S(1)}, f32[3,1,1024]{2,1,0:T(1,128)S(1)}, u32[]{:S(2)}, u32[]{:S(2)}) collective-permute-start(f32[3,1,1024]{2,1,0:T(1,128)S(1)} %get-tuple-element.35), channel_id=1, source_target_pairs={{1,0},{2,1},{3,2},{4,3},{5,4},{6,5},{7,6},{8,7},{9,8},{10,9},{11,1... | collective-permute-start | bytes 36872 | tf_op jit(solution)/shard_map/ppermute | solution.py:25
  72.1 11.0 %collective-permute-start.5 = (f32[3,1,1024]{2,1,0:T(1,128)S(1)}, f32[3,1,1024]{2,1,0:T(1,128)S(1)}, u32[]{:S(2)}, u32[]{:S(2)}) collective-permute-start(f32[3,1,1024]{2,1,0:T(1,128)S(1)} %get-tuple-element.32), channel_id=1, source_target_pairs={{0,1},{1,2},{2,3},{3,4},{4,5},{5,6},{6,7},{7,8},{8,9},{9,10},{10,1... | collective-permute-start | bytes 36872 | tf_op jit(solution)/shard_map/ppermute | solution.py:22
  74.0 10.5 %collective-permute-start.6 = (f32[3,1,1024]{2,1,0:T(1,128)S(1)}, f32[3,1,1024]{2,1,0:T(1,128)S(1)}, u32[]{:S(2)}, u32[]{:S(2)}) collective-permute-start(f32[3,1,1024]{2,1,0:T(1,128)S(1)} %get-tuple-element.33), channel_id=1, source_target_pairs={{1,0},{2,1},{3,2},{4,3},{5,4},{6,5},{7,6},{8,7},{9,8},{10,9},{11,1... | collective-permute-start | bytes 36872 | tf_op jit(solution)/shard_map/ppermute | solution.py:25
  85.2 10.0 %copy-start.3 = (f32[3,16,4096]{2,1,0:T(8,128)S(1)}, f32[3,16,4096]{2,1,0:T(8,128)}, u32[]{:S(2)}) copy-start(f32[3,16,4096]{2,1,0:T(8,128)} %param.4) | copy-start | bytes 2359300
  85.9 13.3 %copy-start.5 = (f32[3,8,1024]{2,1,0:T(8,128)}, f32[3,8,1024]{2,1,0:T(8,128)S(1)}, u32[]{:S(2)}) copy-start(f32[3,8,1024]{2,1,0:T(8,128)S(1)} %add_add_fusion) | copy-start | bytes 294916
  85.9 13.3 %collective-permute-start.7 = (f32[3,1,1024]{2,1,0:T(1,128)S(1)}, f32[3,1,1024]{2,1,0:T(1,128)S(1)}, u32[]{:S(2)}, u32[]{:S(2)}) collective-permute-start(f32[3,1,1024]{2,1,0:T(1,128)S(1)} %slice.319), channel_id=1, source_target_pairs={{1,0},{2,1},{3,2},{4,3},{5,4},{6,5},{7,6},{8,7},{9,8},{10,9},{11,1... | collective-permute-start | bytes 36872 | tf_op jit(solution)/shard_map/ppermute | solution.py:33
where the time goes:
time: 131 us; the launch traced here: 130 us
  local copies, waits for them, and re-layouts  53.7 us (41%)
  starting transfers between devices  47.5 us (36%)
  other arithmetic  16.5 us (13%)
  waiting for transfers between devices  11.1 us (8%)
    ppermute x3, starting transfers between devices, extended_2(): lax.ppermute(lax.slice_in_dim(block, 0, width, axis=dim), axis, backward)  28.3 us
    ppermute x2, starting transfers between devices, passed_along(): return lax.ppermute(block, axis, route)  11.2 us
    unnamed x18, local copies, waits for them, and re-layouts  10.5 us
    slice x2, local copies, waits for them, and re-layouts, restrict_cross(): blocks = blocks[:, :, :, 0::2] + 0.5 * (odd_cols + jnp.roll(odd_cols, 1, 3))  9.86 us
    slice x1, local copies, waits for them, and re-layouts, restrict_cross(): odd_cols = blocks[:, :, :, 1::2]  9.84 us
    another operation x1, local copies, waits for them, and re-layouts, prolong(): jnp.stack([refined, mid_cols], axis=4)  8.53 us
    ppermute x2, waiting for transfers between devices, passed_along(): return lax.ppermute(block, axis, route)  8.32 us
    ppermute x3, starting transfers between devices, extended_2(): lax.ppermute(lax.slice_in_dim(block, block.shape[dim] - width, None, axis...  8.12 us
  transfers between devices with their start and end apart: 8, of which 3 were waited for; matrix products, arithmetic and copies ran while one was open for 5% of the time, Pallas kernels for 0%

commit v1 on v0

v1 whole, which is shorter than its diff:
```python
import jax
import jax.numpy as jnp
from jax import lax
from jax.experimental import pallas as pl
from jax.experimental.pallas import tpu as pltpu
from jax.sharding import PartitionSpec as P

NY = 32
NZ = 32
DEGREE = 3
LOWER_EIG = 0.15
UPPER_EIG = 1.95
CENTER = 0.5 * (UPPER_EIG + LOWER_EIG)
HALF_WIDTH = 0.5 * (UPPER_EIG - LOWER_EIG)

COMPS = 3
FINE = 4 * NY * NZ
COARSE = NY * NZ
PLANES = 16
HALF = PLANES // 2
LANES = 128
BLOCKS = COARSE // LANES
WIDE = FINE // BLOCKS
TILES = FINE // LANES
F32 = jnp.float32
BF16 = jnp.bfloat16


def fill_restrict(ref):
    fine = lax.broadcasted_iota(jnp.int32, (2 * NZ, LANES), 0)
    lane = lax.broadcasted_iota(jnp.int32, (2 * NZ, LANES), 1)
    apart = (fine - 2 * (lane % NZ) + 2 * NZ) % (2 * NZ)
    cols = jnp.where(apart == 0, 1.0, jnp.where((apart == 1) | (apart == 2 * NZ - 1), 0.5, 0.0))
    for row in range(8):
        away = jnp.abs(2 * (lane // NZ) - row)
        rows = jnp.where(away == 0, 1.0, jnp.where(away == 1, 0.5, 0.0))
        at = slice(2 * NZ * row, 2 * NZ * (row + 1))
        ref[at, :LANES] = (cols * rows).astype(BF16)
        beyond = jnp.where(lane < NZ, 0.5 * cols, 0.0) if row == 7 else jnp.zeros_like(cols)
        ref[at, LANES:] = beyond.astype(BF16)


def fill_prolong(ref):
    coarse = lax.broadcasted_iota(jnp.int32, (NZ, LANES), 0)
    lane = lax.broadcasted_iota(jnp.int32, (NZ, LANES), 1)
    apart = (lane - 2 * coarse + 2 * NZ) % (2 * NZ)
    cols = jnp.where(apart == 0, 1.0, jnp.where((apart == 1) | (apart == 2 * NZ - 1), 0.5, 0.0))
    for row in range(8):
        for part in range(4):
            away = jnp.abs(2 * row - 2 * part - lane // (2 * NZ))
            rows = jnp.where(away == 0, 1.0, jnp.where(away == 1, 0.5, 0.0))
            kept = cols * rows if row < 5 else jnp.zeros_like(cols)
            ref[NZ * row : NZ * (row + 1), tile(part)] = kept.astype(BF16)


def split_dot(left, matrix):
    high = left.astype(BF16)
    low = (left - high.astype(F32)).astype(BF16)
    return jnp.dot(high, matrix, preferred_element_type=F32) + jnp.dot(
        low, matrix, preferred_element_type=F32
    )


def restricted(blocks, matrix):
    sums = split_dot(jnp.concatenate(blocks, axis=0), matrix)
    parts = [sums[PLANES * s : PLANES * (s + 1)] for s in range(BLOCKS)]
    return [parts[s][:, :LANES] + parts[s - 1][:, LANES:] for s in range(BLOCKS)]


def iotas(rows):
    row = lax.broadcasted_iota(jnp.int32, (rows, LANES), 0)
    lane = lax.broadcasted_iota(jnp.int32, (rows, LANES), 1)
    return row, lane


def tile(index):
    return slice(LANES * index, LANES * (index + 1))


def local_kernel(
    v_hbm, f_hbm, c_hbm, cv_ref, s_ref, l_ref, src_ref, w_ref, v_vm, f_vm, c_vm, cross_vm, sems
):
    copies = [pltpu.make_async_copy(c_hbm, c_vm, sems.at[0])]
    for k in range(COMPS):
        copies.append(pltpu.make_async_copy(v_hbm.at[k], v_vm.at[k], sems.at[1 + 2 * k]))
        copies.append(pltpu.make_async_copy(f_hbm.at[k], f_vm.at[k], sems.at[2 + 2 * k]))
    for copy in copies:
        copy.start()

    odd = lax.rem(lax.axis_index("sub"), 2)
    even_device = odd == 0
    s_plane = (PLANES - 1) * (1 - odd)
    l_plane = (PLANES - 1) * odd
    row, lane = iotas(PLANES)
    low_half = lane < 64
    first_col = lane % 64 == 0
    last_col = lane % 64 == 63
    row8, _ = iotas(HALF)
    fill_restrict(w_ref)
    matrix = w_ref[...]

    def send(tile_at, to_right, to_left):
        s_ref[4:8, tile(tile_at)] = jnp.where(even_device, to_right, to_left)[4:8]
        l_ref[4:8, tile(tile_at)] = jnp.where(even_device, to_left, to_right)[4:8]

    for t in range(BLOCKS):
        part = cv_ref[:, tile(t)]
        send(COMPS * BLOCKS + t, pltpu.roll(part, 6, 0), pltpu.roll(part, 4, 0))

    copies[0].wait()
    s_ref[3:4, :] = c_vm[pl.ds(s_plane, 1), :]
    l_ref[3:4, :] = c_vm[pl.ds(l_plane, 1), :]

    for k in range(COMPS):
        copies[1 + 2 * k].wait()
        copies[2 + 2 * k].wait()
        swapped = [pltpu.roll(v_vm[k, :, tile(t)], 64, 1) for t in range(TILES)]
        blocks = []
        for s in range(BLOCKS):
            pieces = []
            for t in range(4 * s, 4 * s + 4):
                x = v_vm[k, :, tile(t)]
                coeff = c_vm[:, tile(t)]
                turned = swapped[t]
                beside = turned + jnp.where(low_half, swapped[t - 1], swapped[(t + 1) % TILES])
                beside += pltpu.roll(jnp.where(last_col, turned, x), 1, 1)
                beside += pltpu.roll(jnp.where(first_col, turned, x), LANES - 1, 1)
                beside += jnp.where(row == 0, 0.0, pltpu.roll(x, 1, 0))
                beside += jnp.where(row == PLANES - 1, 0.0, pltpu.roll(x, PLANES - 1, 0))
                pieces.append(f_vm[k, :, tile(t)] - x + coeff * (beside - 6.0 * x))
            blocks.append(jnp.concatenate(pieces, axis=1))
        crossed = restricted(blocks, matrix)
        for t in range(BLOCKS):
            cross_vm[k * BLOCKS + t] = crossed[t]
        for t in range(BLOCKS):
            evens = cross_vm[k * BLOCKS + t, pl.ds(0, HALF, 2), :]
            odds = 0.0625 * cross_vm[k * BLOCKS + t, pl.ds(1, HALF, 2), :]
            source = 0.125 * evens + odds + jnp.where(row8 == 0, 0.0, pltpu.roll(odds, 1, 0))
            src_ref[k, :, tile(t)] = source
            to_right = jnp.where(row8 == 6, pltpu.roll(odds, 7, 0), pltpu.roll(source, 6, 0))
            send(k * BLOCKS + t, to_right, pltpu.roll(source, 4, 0))
        s_ref[k : k + 1, :] = v_vm[k, pl.ds(s_plane, 1), :]
        l_ref[k : k + 1, :] = v_vm[k, pl.ds(l_plane, 1), :]


def near_sum(tiles, lane):
    ups = [pltpu.roll(x, LANES - NZ, 1) for x in tiles]
    downs = [pltpu.roll(x, NZ, 1) for x in tiles]
    sums = []
    for s, x in enumerate(tiles):
        total = jnp.where(lane < LANES - NZ, ups[s], ups[(s + 1) % BLOCKS])
        total += jnp.where(lane >= NZ, downs[s], downs[s - 1])
        total += pltpu.roll(jnp.where(lane % NZ == NZ - 1, ups[s], x), 1, 1)
        total += pltpu.roll(jnp.where(lane % NZ == 0, downs[s], x), LANES - 1, 1)
        total += pltpu.roll(x, 1, 0) + pltpu.roll(x, PLANES - 1, 0)
        sums.append(total)
    return sums


def finish_kernel(
    v_hbm,
    cv_ref,
    src_ref,
    s_sent,
    l_sent,
    s_got,
    l_got,
    out_hbm,
    fix_ref,
    w_ref,
    q_ref,
    v_vm,
    out_vm,
    mix_vm,
    in_sems,
    out_sems,
):
    loads = [pltpu.make_async_copy(v_hbm.at[k], v_vm.at[k], in_sems.at[k]) for k in range(COMPS)]
    for load in loads:
        load.start()

    even_device = lax.rem(lax.axis_index("sub"), 2) == 0
    _, lane = iotas(PLANES)
    row8, _ = iotas(HALF)
    fill_restrict(w_ref)
    fill_prolong(q_ref)
    matrix = w_ref[...]
    spread = q_ref[...]

    def coupling(sent, got):
        blocks = []
        for s in range(BLOCKS):
            at = slice(WIDE * s, WIDE * (s + 1))
            theirs = got[:, at] * sent[3:4, at]
            ours = sent[:, at] * got[3:4, at]
            blocks.append(jnp.concatenate([theirs, ours], axis=0))
        return restricted(blocks, matrix)

    s_terms = coupling(s_sent, s_got)
    l_terms = coupling(l_sent, l_got)

    def sides(at):
        s_part, l_part = s_got[:, at], l_got[:, at]
        left = jnp.where(even_device, l_part, s_part)
        right = jnp.where(even_device, s_part, l_part)
        above = jnp.where(row8 >= 6, pltpu.roll(left, 2, 0), 0.0)
        below = jnp.where(row8 <= 2, pltpu.roll(right, 4, 0), 0.0)
        return pltpu.roll(left, 2, 0), above + below

    quotients, inverses, inside = [], [], []
    for t in range(BLOCKS):
        _, outer = sides(tile(COMPS * BLOCKS + t))
        coeff = jnp.concatenate([cv_ref[:, tile(t)], outer], axis=0)
        inverse = 1.0 / (1.0 + 6.0 * coeff)
        inverses.append(inverse)
        quotients.append(coeff * inverse)
        inside.append(outer > 0.0)

    sigma = CENTER / HALF_WIDTH
    stores = []
    for k in range(COMPS):
        scaled = []
        for t in range(BLOCKS):
            at = tile(k * BLOCKS + t)
            left_turned, outer = sides(at)
            own_right = pltpu.roll(jnp.where(even_device, s_sent[:, at], l_sent[:, at]), 2, 0)
            left_terms = jnp.where(even_device, l_terms[t], s_terms[t])
            right_terms = jnp.where(even_device, s_terms[t], l_terms[t])
            left_got, left_own = left_terms[k : k + 1], left_terms[HALF + k : HALF + k + 1]
            right_got, right_own = right_terms[k : k + 1], right_terms[HALF + k : HALF + k + 1]
            first = left_turned + (0.125 * left_got + 0.0625 * left_own)
            inner = src_ref[k, :, tile(t)] + jnp.where(row8 == 0, first, 0.0)
            inner += jnp.where(row8 == HALF - 1, 0.0625 * right_got, 0.0)
            after = own_right + (0.0625 * right_got + 0.125 * right_own)
            outer += jnp.where(row8 == 0, after, 0.0)
            outer += jnp.where(row8 == HALF - 1, 0.0625 * left_own, 0.0)
            outer = jnp.where(inside[t], outer, 0.0)
            scaled.append(jnp.concatenate([inner, outer], axis=0) * inverses[t])

        update = [x * (1.0 / CENTER) for x in scaled]
        approx = update
        ratio_old = 1.0 / sigma
        for _ in range(DEGREE - 1):
            ratio_new = 1.0 / (2.0 * sigma - ratio_old)
            keep, gain = ratio_new * ratio_old, 2.0 * ratio_new / HALF_WIDTH
            sums = near_sum(approx, lane)
            update = [
                keep * update[t] + gain * (scaled[t] - approx[t] + quotients[t] * sums[t])
                for t in range(BLOCKS)
            ]
            approx = [approx[t] + update[t] for t in range(BLOCKS)]
            ratio_old = ratio_new

        for t in range(BLOCKS):
            own = approx[t][:HALF]
            fix_ref[k, :, tile(t)] = own
            mix_vm[k * BLOCKS + t, pl.ds(0, HALF, 2), :] = own
            mix_vm[k * BLOCKS + t, pl.ds(1, HALF, 2), :] = 0.5 * (own + pltpu.roll(approx[t], PLANES - 1, 0)[:HALF])
        mixed = [mix_vm[k * BLOCKS + t] for t in range(BLOCKS)]
        pairs = [jnp.concatenate([mixed[s], mixed[(s + 1) % BLOCKS]], axis=1) for s in range(BLOCKS)]
        fine = split_dot(jnp.concatenate(pairs, axis=0), spread)
        loads[k].wait()
        for s in range(BLOCKS):
            at = slice(WIDE * s, WIDE * (s + 1))
            out_vm[k, :, at] = v_vm[k, :, at] + fine[PLANES * s : PLANES * (s + 1)]
        store = pltpu.make_async_copy(out_vm.at[k], out_hbm.at[k], out_sems.at[k])
        store.start()
        stores.append(store)
    for store in stores:
        store.wait()


VMEM = pl.BlockSpec(memory_space=pltpu.VMEM)
ANY = pl.BlockSpec(memory_space=pl.ANY)
LIMIT = 16 * 2**20


def shards(velocity, forcing, viscosity, coarse_visc):
    message = jax.ShapeDtypeStruct((8, FINE), F32)
    s_sent, l_sent, source = pl.pallas_call(
        local_kernel,
        out_shape=(message, message, jax.ShapeDtypeStruct((COMPS, HALF, COARSE), F32)),
        in_specs=[ANY, ANY, ANY, VMEM],
        out_specs=(VMEM, VMEM, VMEM),
        scratch_shapes=[
            pltpu.VMEM((WIDE, 2 * LANES), BF16),
            pltpu.VMEM((COMPS, PLANES, FINE), F32),
            pltpu.VMEM((COMPS, PLANES, FINE), F32),
            pltpu.VMEM((PLANES, FINE), F32),
            pltpu.VMEM((COMPS * BLOCKS, PLANES, LANES), F32),
            pltpu.SemaphoreType.DMA((1 + 2 * COMPS,)),
        ],
        compiler_params=pltpu.CompilerParams(vmem_limit_bytes=LIMIT),
    )(velocity, forcing, viscosity, coarse_visc)

    axes = ("grp", "sub")
    count = lax.axis_size(axes)
    far = [(i, i + 1) for i in range(1, count - 1, 2)]
    near = [(i, i + 1) for i in range(0, count, 2)]
    l_got = lax.ppermute(l_sent, axes, far + [(j, i) for i, j in far])
    s_got = lax.ppermute(s_sent, axes, near + [(j, i) for i, j in near])

    return pl.pallas_call(
        finish_kernel,
        out_shape=(
            jax.ShapeDtypeStruct(velocity.shape, F32),
            jax.ShapeDtypeStruct((COMPS, HALF, COARSE), F32),
        ),
        in_specs=[ANY] + [VMEM] * 6,
        out_specs=(ANY, VMEM),
        scratch_shapes=[
            pltpu.VMEM((WIDE, 2 * LANES), BF16),
            pltpu.VMEM((2 * LANES, WIDE), BF16),
            pltpu.VMEM((COMPS, PLANES, FINE), F32),
            pltpu.VMEM((COMPS, PLANES, FINE), F32),
            pltpu.VMEM((COMPS * BLOCKS, PLANES, LANES), F32),
            pltpu.SemaphoreType.DMA((COMPS,)),
            pltpu.SemaphoreType.DMA((COMPS,)),
        ],
        compiler_params=pltpu.CompilerParams(vmem_limit_bytes=LIMIT),
    )(velocity, coarse_visc, source, s_sent, l_sent, s_got, l_got)


def solution(mesh):
    return jax.shard_map(
        shards,
        mesh=mesh,
        in_specs=(
            P(None, ("grp", "sub"), None),
            P(None, ("grp", "sub"), None),
            P(("grp", "sub"), None),
            P(("grp", "sub"), None),
        ),
        out_specs=(P(None, ("grp", "sub"), None), P(None, ("grp", "sub"), None)),
        check_vma=False,
    )
```

time: 131 us -> 28.5 us (0.22)
  the two profiles are of different devices: /device:TPU:32 before, /device:TPU:56 now
where the time goes in v1:
time: 28.5 us; the launch traced here: 28.2 us
  starting transfers between devices  15.5 us (54%)
  Pallas kernels  5.24 us (18%)
  local copies, waits for them, and re-layouts  3.97 us (14%)
  waiting for transfers between devices  2.73 us (10%)
  between operations  0.67 us (2%)
    ppermute x1, starting transfers between devices, shards(): l_got = lax.ppermute(l_sent, axes, far + [(j, i) for i, j in far])  11.3 us
    ppermute x1, starting transfers between devices, shards(): s_got = lax.ppermute(s_sent, axes, near + [(j, i) for i, j in near])  4.28 us
    unnamed x8, local copies, waits for them, and re-layouts  3.97 us
    pallas_call x1, Pallas kernels, shards(): pl.pallas_call(finish_kernel, out_shape=(jax.ShapeDtypeStruct(velocity.sh...  3.43 us
    ppermute x1, waiting for transfers between devices, shards(): l_got = lax.ppermute(l_sent, axes, far + [(j, i) for i, j in far])  2.73 us
    pallas_call x1, Pallas kernels, shards(): pl.pallas_call(local_kernel, out_shape=(message, message, jax.ShapeDtypeS...  1.81 us
  transfers between devices with their start and end apart: 2, of which 1 were waited for; matrix products, arithmetic and copies ran while one was open for 0% of the time, Pallas kernels for 0%

profile of v1, /device:TPU:56, one launch (start us, length us, event | category | flops | bytes accessed | tf_op | source)
XLA Modules:
  0.0 28.2 jit_solution(17380343947817593285)
XLA Ops:
  0.6 0.0 copy-start
  0.6 1.1 %copy-done = f32[3,16,4096]{2,1,0:T(8,128)S(1)} copy-done((f32[3,16,4096]{2,1,0:T(8,128)S(1)}, f32[3,16,4096]{2,1,0:T(8,128)}, u32[]{:S(2)}) %copy-start) | copy-done | bytes 786456
  1.8 0.0 copy-start.1
  1.8 1.1 %copy-done.1 = f32[3,16,4096]{2,1,0:T(8,128)S(1)} copy-done((f32[3,16,4096]{2,1,0:T(8,128)S(1)}, f32[3,16,4096]{2,1,0:T(8,128)}, u32[]{:S(2)}) %copy-start.1) | copy-done | bytes 786456
  2.9 0.0 copy-start.2
  2.9 0.9 %copy-done.2 = f32[16,4096]{1,0:T(8,128)S(1)} copy-done((f32[16,4096]{1,0:T(8,128)S(1)}, f32[16,4096]{1,0:T(8,128)}, u32[]{:S(2)}) %copy-start.2) | copy-done | bytes 262168
  3.8 0.0 copy-start.3
  3.9 0.8 %copy-done.3 = f32[8,1024]{1,0:T(8,128)S(1)} copy-done((f32[8,1024]{1,0:T(8,128)S(1)}, f32[8,1024]{1,0:T(8,128)}, u32[]{:S(2)}) %copy-start.3) | copy-done | bytes 32792
  4.6 1.8 %shard_map.59 = (f32[8,4096]{1,0:T(8,128)S(1)}, f32[8,4096]{1,0:T(8,128)S(1)}, f32[3,8,1024]{2,1,0:T(8,128)S(1)}) custom-call(f32[3,16,4096]{2,1,0:T(8,128)S(1)} %copy-done, f32[3,16,4096]{2,1,0:T(8,128)S(1)} %copy-done.1, f32[16,4096]{1,0:T(8,128)S(1)} %copy-done.2, f32[8,1024]{1,0:T(8,128)S(1)} %copy-done.3), custom_call_target="tpu_custom_call" | custom-call | tf_op jit(solution)/shard_map/pallas_call | solution.py:280
  6.4 4.3 %collective-permute-start = (f32[8,4096]{1,0:T(8,128)S(1)}, f32[8,4096]{1,0:T(8,128)S(1)}, u32[]{:S(2)}, u32[]{:S(2)}) collective-permute-start(f32[8,4096]{1,0:T(8,128)S(1)} %get-tuple-element.6.s_sent), channel_id=1, source_target_pairs={{0,1},{2,3},{4,5},{6,7},{8,9},{10,11},{12,13},{14,15},{16,17},{18,... | collective-permute-start | bytes 393224 | tf_op jit(solution)/shard_map/ppermute | solution.py:301
  10.7 11.3 %collective-permute-start.1 = (f32[8,4096]{1,0:T(8,128)S(1)}, f32[8,4096]{1,0:T(8,128)S(1)}, u32[]{:S(2)}, u32[]{:S(2)}) collective-permute-start(f32[8,4096]{1,0:T(8,128)S(1)} %get-tuple-element.7.l_sent), channel_id=1, source_target_pairs={{1,2},{3,4},{5,6},{7,8},{9,10},{11,12},{13,14},{15,16},{17,18},{19... | collective-permute-start | bytes 393224 | tf_op jit(solution)/shard_map/ppermute | solution.py:300
  22.0 0.0 collective-permute-done.s_got
  22.0 2.7 %collective-permute-done.1.l_got = f32[8,4096]{1,0:T(8,128)S(1)} collective-permute-done((f32[8,4096]{1,0:T(8,128)S(1)}, f32[8,4096]{1,0:T(8,128)S(1)}, u32[]{:S(2)}, u32[]{:S(2)}) %collective-permute-start.1) | collective-permute-done | bytes 131104 | tf_op jit(solution)/shard_map/ppermute | solution.py:300
  24.7 3.4 %shard_map.60 = (f32[3,16,4096]{2,1,0:T(8,128)}, f32[3,8,1024]{2,1,0:T(8,128)}) custom-call(f32[3,16,4096]{2,1,0:T(8,128)S(1)} %copy-done, f32[8,1024]{1,0:T(8,128)S(1)} %copy-done.3, f32[3,8,1024]{2,1,0:T(8,128)S(1)} %get-tuple-element.5.src_ref, f32[8,4096]{1,0:T(8,128)S(1)} %get-tuple-element.6.s_sent, f32[8,4096]{1,0:T(8,128)S(1)} %get-tuple-element.7.l_sent, ...), custom_call_target="tpu_custom_call" | custom-call | tf_op jit(solution)/shard_map/pallas_call | solution.py:303
Async XLA Ops:
  0.6 1.1 %copy-start = (f32[3,16,4096]{2,1,0:T(8,128)S(1)}, f32[3,16,4096]{2,1,0:T(8,128)}, u32[]{:S(2)}) copy-start(f32[3,16,4096]{2,1,0:T(8,128)} %v_hbm.3) | copy-start | bytes 2359300
  1.8 1.1 %copy-start.1 = (f32[3,16,4096]{2,1,0:T(8,128)S(1)}, f32[3,16,4096]{2,1,0:T(8,128)}, u32[]{:S(2)}) copy-start(f32[3,16,4096]{2,1,0:T(8,128)} %f_hbm.1) | copy-start | bytes 2359300
  2.9 0.9 %copy-start.2 = (f32[16,4096]{1,0:T(8,128)S(1)}, f32[16,4096]{1,0:T(8,128)}, u32[]{:S(2)}) copy-start(f32[16,4096]{1,0:T(8,128)} %c_hbm.1) | copy-start | bytes 786436
  3.8 0.8 %copy-start.3 = (f32[8,1024]{1,0:T(8,128)S(1)}, f32[8,1024]{1,0:T(8,128)}, u32[]{:S(2)}) copy-start(f32[8,1024]{1,0:T(8,128)} %cv_ref.3) | copy-start | bytes 98308
  6.4 15.6 %collective-permute-start = (f32[8,4096]{1,0:T(8,128)S(1)}, f32[8,4096]{1,0:T(8,128)S(1)}, u32[]{:S(2)}, u32[]{:S(2)}) collective-permute-start(f32[8,4096]{1,0:T(8,128)S(1)} %get-tuple-element.6.s_sent), channel_id=1, source_target_pairs={{0,1},{2,3},{4,5},{6,7},{8,9},{10,11},{12,13},{14,15},{16,17},{18,... | collective-permute-start | bytes 393224 | tf_op jit(solution)/shard_map/ppermute | solution.py:301
  10.7 14.0 %collective-permute-start.1 = (f32[8,4096]{1,0:T(8,128)S(1)}, f32[8,4096]{1,0:T(8,128)S(1)}, u32[]{:S(2)}, u32[]{:S(2)}) collective-permute-start(f32[8,4096]{1,0:T(8,128)S(1)} %get-tuple-element.7.l_sent), channel_id=1, source_target_pairs={{1,2},{3,4},{5,6},{7,8},{9,10},{11,12},{13,14},{15,16},{17,18},{19... | collective-permute-start | bytes 393224 | tf_op jit(solution)/shard_map/ppermute | solution.py:300

commit v2 on v1

v2 whole, which is shorter than its diff:
```python
import jax
import jax.numpy as jnp
from jax import lax
from jax.experimental import pallas as pl
from jax.experimental.pallas import tpu as pltpu
from jax.sharding import PartitionSpec as P

NY = 32
NZ = 32
DEGREE = 3
LOWER_EIG = 0.15
UPPER_EIG = 1.95
CENTER = 0.5 * (UPPER_EIG + LOWER_EIG)
HALF_WIDTH = 0.5 * (UPPER_EIG - LOWER_EIG)

COMPS = 3
FINE = 4 * NY * NZ
COARSE = NY * NZ
PLANES = 16
HALF = PLANES // 2
LANES = 128
BLOCKS = COARSE // LANES
WIDE = FINE // BLOCKS
TILES = FINE // LANES
F32 = jnp.float32
BF16 = jnp.bfloat16


def tile(index):
    return slice(LANES * index, LANES * (index + 1))


def fill_restrict(ref):
    fine = lax.broadcasted_iota(jnp.int32, (2 * NZ, LANES), 0)
    lane = lax.broadcasted_iota(jnp.int32, (2 * NZ, LANES), 1)
    apart = (fine - 2 * (lane % NZ) + 2 * NZ) % (2 * NZ)
    cols = jnp.where(apart == 0, 1.0, jnp.where((apart == 1) | (apart == 2 * NZ - 1), 0.5, 0.0))
    for row in range(8):
        away = jnp.abs(2 * (lane // NZ) - row)
        rows = jnp.where(away == 0, 1.0, jnp.where(away == 1, 0.5, 0.0))
        at = slice(2 * NZ * row, 2 * NZ * (row + 1))
        ref[at, :LANES] = (cols * rows).astype(BF16)
        beyond = jnp.where(lane < NZ, 0.5 * cols, 0.0) if row == 7 else jnp.zeros_like(cols)
        ref[at, LANES:] = beyond.astype(BF16)


def fill_prolong(ref):
    coarse = lax.broadcasted_iota(jnp.int32, (NZ, LANES), 0)
    lane = lax.broadcasted_iota(jnp.int32, (NZ, LANES), 1)
    apart = (lane - 2 * coarse + 2 * NZ) % (2 * NZ)
    cols = jnp.where(apart == 0, 1.0, jnp.where((apart == 1) | (apart == 2 * NZ - 1), 0.5, 0.0))
    for row in range(8):
        for part in range(4):
            away = jnp.abs(2 * row - 2 * part - lane // (2 * NZ))
            rows = jnp.where(away == 0, 1.0, jnp.where(away == 1, 0.5, 0.0))
            kept = cols * rows if row < 5 else jnp.zeros_like(cols)
            ref[NZ * row : NZ * (row + 1), tile(part)] = kept.astype(BF16)


def split_dot(left, matrix):
    high = left.astype(BF16)
    low = (left - high.astype(F32)).astype(BF16)
    return jnp.dot(high, matrix, preferred_element_type=F32) + jnp.dot(
        low, matrix, preferred_element_type=F32
    )


def iotas(rows):
    row = lax.broadcasted_iota(jnp.int32, (rows, LANES), 0)
    lane = lax.broadcasted_iota(jnp.int32, (rows, LANES), 1)
    return row, lane


def eight(index):
    return slice(8 * index, 8 * (index + 1))


def local_kernel(
    v_hbm,
    f_hbm,
    c_hbm,
    cv_hbm,
    right_ref,
    left_ref,
    src_ref,
    v_ref,
    cv_ref,
    w_ref,
    q_ref,
    f_vm,
    c_vm,
    cross_vm,
    sems,
):
    copies = [pltpu.make_async_copy(c_hbm, c_vm, sems.at[0])]
    for k in range(COMPS):
        copies.append(pltpu.make_async_copy(v_hbm.at[k], v_ref.at[k], sems.at[1 + 2 * k]))
        copies.append(pltpu.make_async_copy(f_hbm.at[k], f_vm.at[k], sems.at[2 + 2 * k]))
    copies.append(pltpu.make_async_copy(cv_hbm, cv_ref, sems.at[1 + 2 * COMPS]))
    for copy in copies:
        copy.start()

    row, lane = iotas(PLANES)
    low_half = lane < 64
    first_col = lane % 64 == 0
    last_col = lane % 64 == 63
    fill_restrict(w_ref)
    fill_prolong(q_ref)
    matrix = w_ref[...]

    def packed_planes(slab, source):
        for part in range(4):
            left_ref[slab, :, tile(part)] = source[0, pl.ds(8 * part, 8, 32), :]
            right_ref[slab, :, tile(part)] = source[1, pl.ds(8 * part + 7, 8, 32), :]

    copies[0].wait()
    packed_planes(COMPS, c_vm)

    for k in range(COMPS):
        copies[1 + 2 * k].wait()
        copies[2 + 2 * k].wait()

        def planes_of(ref, t):
            return jnp.concatenate([ref[0, eight(t), :], ref[1, eight(t), :]], axis=0)

        values = [planes_of(v_ref.at[k], t) for t in range(TILES)]
        swapped = [pltpu.roll(x, 64, 1) for x in values]
        blocks = []
        for s in range(BLOCKS):
            pieces = []
            for t in range(4 * s, 4 * s + 4):
                x, turned = values[t], swapped[t]
                beside = turned + jnp.where(low_half, swapped[t - 1], swapped[(t + 1) % TILES])
                beside += pltpu.roll(jnp.where(last_col, turned, x), 1, 1)
                beside += pltpu.roll(jnp.where(first_col, turned, x), LANES - 1, 1)
                beside += jnp.where(row == 0, 0.0, pltpu.roll(x, 1, 0))
                beside += jnp.where(row == PLANES - 1, 0.0, pltpu.roll(x, PLANES - 1, 0))
                pieces.append(
                    planes_of(f_vm.at[k], t) - x + planes_of(c_vm, t) * (beside - 6.0 * x)
                )
            blocks.append(jnp.concatenate(pieces, axis=1))
        sums = split_dot(jnp.concatenate(blocks, axis=0), matrix)
        parts = [sums[PLANES * s : PLANES * (s + 1)] for s in range(BLOCKS)]
        for s in range(BLOCKS):
            crossed = parts[s][:, :LANES] + parts[s - 1][:, LANES:]
            cross_vm[k, PLANES * s : PLANES * (s + 1), :] = crossed
        planes = [cross_vm[k, pl.ds(p, 8, PLANES), :] for p in range(PLANES)]
        half_odds = [0.0625 * planes[2 * j + 1] for j in range(HALF)]
        sources = []
        for j in range(HALF):
            source = 0.125 * planes[2 * j] + half_odds[j]
            if j > 0:
                source += half_odds[j - 1]
            src_ref[k, eight(j), :] = source
            sources.append(source)
        for j in range(3):
            left_ref[4 + j, :, tile(k)] = sources[j]
            right_ref[4 + j, :, tile(k)] = (sources[6:] + half_odds[-1:])[j]
        packed_planes(k, v_ref.at[k])

    copies[-1].wait()
    for j in range(3):
        left_ref[4 + j, :, tile(COMPS)] = cv_ref[pl.ds(j, 8, 8), :]
        right_ref[4 + j, :, tile(COMPS)] = cv_ref[pl.ds(min(6 + j, 7), 8, 8), :]


def finish_kernel(
    v_ref,
    cv_ref,
    src_ref,
    right_sent,
    left_sent,
    right_got,
    left_got,
    w_ref,
    q_ref,
    out_hbm,
    fix_ref,
    out_vm,
    mix_vm,
    sems,
):
    _, lane = iotas(8)
    kept_up = lane < LANES - NZ
    kept_down = lane >= NZ
    first_col = lane % NZ == 0
    last_col = lane % NZ == NZ - 1

    rows = []
    for sent, got in ((left_sent, right_got), (right_sent, left_got)):
        rows += [got[k] * sent[COMPS] for k in range(COMPS)]
        rows += [sent[k] * got[COMPS] for k in range(COMPS)]
    sums = split_dot(jnp.concatenate(rows, axis=0), w_ref[...])
    terms = []
    for part in range(len(rows)):
        mine = sums[eight(part)]
        terms.append(mine[:, :LANES] + pltpu.roll(mine[:, LANES:], 1, 0))

    first, last = -2, HALF + 2
    inverse, quotient = {}, {}
    for j in range(first, last + 1):
        if j < 0:
            coeff = right_got[6 + j, :, tile(COMPS)]
        elif j < HALF:
            coeff = cv_ref[pl.ds(j, 8, 8), :]
        else:
            coeff = left_got[4 + j - HALF, :, tile(COMPS)]
        if j == HALF:
            inside = coeff > 0.0
        inverse[j] = 1.0 / (1.0 + 6.0 * coeff)
        quotient[j] = coeff * inverse[j]

    def near_sum(planes, j):
        x = planes[j]
        up = pltpu.roll(x, LANES - NZ, 1)
        down = pltpu.roll(x, NZ, 1)
        total = planes[j - 1] + planes[j + 1]
        total += jnp.where(kept_up, up, pltpu.roll(up, 7, 0))
        total += jnp.where(kept_down, down, pltpu.roll(down, 1, 0))
        total += pltpu.roll(jnp.where(last_col, up, x), 1, 1)
        total += pltpu.roll(jnp.where(first_col, down, x), LANES - 1, 1)
        return total

    sigma = CENTER / HALF_WIDTH
    stores = []
    for k in range(COMPS):
        at = tile(k)
        left_theirs, left_ours = terms[k], terms[COMPS + k]
        right_theirs, right_ours = terms[2 * COMPS + k], terms[3 * COMPS + k]
        source = {j: src_ref[k, eight(j), :] for j in range(HALF)}
        source[-2] = right_got[4, :, at]
        source[-1] = right_got[5, :, at] + 0.0625 * left_ours
        source[0] += right_got[6, :, at] + (0.125 * left_theirs + 0.0625 * left_ours)
        source[HALF - 1] += 0.0625 * right_theirs
        after = right_sent[6, :, at] + left_got[4, :, at] + (0.0625 * right_theirs + 0.125 * right_ours)
        source[HALF] = jnp.where(inside, after, 0.0)
        source[HALF + 1] = left_got[5, :, at]
        source[HALF + 2] = left_got[6, :, at]

        scaled = {j: source[j] * inverse[j] for j in source}
        update = {j: x * (1.0 / CENTER) for j, x in scaled.items()}
        approx = update
        ratio_old = 1.0 / sigma
        for sweep in range(1, DEGREE):
            ratio_new = 1.0 / (2.0 * sigma - ratio_old)
            keep, gain = ratio_new * ratio_old, 2.0 * ratio_new / HALF_WIDTH
            inner = range(first + sweep, last - sweep + 1)
            update = {
                j: keep * update[j]
                + gain * (scaled[j] - approx[j] + quotient[j] * near_sum(approx, j))
                for j in inner
            }
            approx = {j: approx[j] + update[j] for j in inner}
            ratio_old = ratio_new

        for j in range(HALF):
            fix_ref[k, pl.ds(j, 8, 8), :] = approx[j]
            mix_vm[k, eight(2 * j), :] = approx[j]
            mix_vm[k, eight(2 * j + 1), :] = 0.5 * (approx[j] + approx[j + 1])
        mixed = [
            [mix_vm[k, pl.ds(64 * h + s, 8, 8), :] for s in range(BLOCKS)] for h in range(2)
        ]
        left = [
            jnp.concatenate([mixed[h][s], mixed[h][(s + 1) % BLOCKS]], axis=1)
            for h in range(2)
            for s in range(BLOCKS)
        ]
        fine = split_dot(jnp.concatenate(left, axis=0), q_ref[...])
        for h in range(2):
            for t in range(TILES):
                add = fine[eight(BLOCKS * h + t // 4), tile(t % 4)]
                out_vm[k, h, eight(t), :] = v_ref[k, h, eight(t), :] + add
        store = pltpu.make_async_copy(out_vm.at[k], out_hbm.at[k], sems.at[k])
        store.start()
        stores.append(store)
    for store in stores:
        store.wait()


VMEM = pl.BlockSpec(memory_space=pltpu.VMEM)
HBM = pl.BlockSpec(memory_space=pltpu.HBM)
LIMIT = 16 * 2**20
FINE_TILED = (2, 8 * TILES, LANES)


def fine_tiled(field):
    lead = field.shape[:-2]
    split = field.reshape(lead + (2, 8, TILES, LANES))
    return jnp.swapaxes(split, -3, -2).reshape(lead + FINE_TILED)


def pinned(field):
    return pltpu.with_memory_space_constraint(fine_tiled(field), pltpu.HBM)


def shards(velocity, forcing, viscosity, coarse_visc):
    coeffs = jnp.swapaxes(coarse_visc.reshape(HALF, BLOCKS, LANES), 0, 1).reshape(8 * HALF, LANES)
    coeffs = pltpu.with_memory_space_constraint(coeffs, pltpu.HBM)
    message = jax.ShapeDtypeStruct((7, 8, WIDE), F32)
    fine = jax.ShapeDtypeStruct((COMPS,) + FINE_TILED, F32)
    coarse = jax.ShapeDtypeStruct((COMPS, 8 * HALF, LANES), F32)
    right_sent, left_sent, source, kept, coeffs, restrict, prolong = pl.pallas_call(
        local_kernel,
        out_shape=(
            message,
            message,
            coarse,
            fine,
            jax.ShapeDtypeStruct((8 * HALF, LANES), F32),
            jax.ShapeDtypeStruct((WIDE, 2 * LANES), BF16),
            jax.ShapeDtypeStruct((2 * LANES, WIDE), BF16),
        ),
        in_specs=[HBM] * 4,
        out_specs=(VMEM,) * 7,
        scratch_shapes=[
            pltpu.VMEM((COMPS,) + FINE_TILED, F32),
            pltpu.VMEM(FINE_TILED, F32),
            pltpu.VMEM((COMPS, 8 * PLANES, LANES), F32),
            pltpu.SemaphoreType.DMA((2 + 2 * COMPS,)),
        ],
        compiler_params=pltpu.CompilerParams(vmem_limit_bytes=LIMIT),
    )(pinned(velocity), pinned(forcing), pinned(viscosity), coeffs)

    axes = ("grp", "sub")
    count = lax.axis_size(axes)
    forward = [(i, i + 1) for i in range(count - 1)]
    right_got = lax.ppermute(right_sent, axes, forward)
    left_got = lax.ppermute(left_sent, axes, [(j, i) for i, j in forward])

    corrected, fix = pl.pallas_call(
        finish_kernel,
        out_shape=(fine, coarse),
        in_specs=[VMEM] * 9,
        out_specs=(HBM, VMEM),
        scratch_shapes=[
            pltpu.VMEM((COMPS,) + FINE_TILED, F32),
            pltpu.VMEM((COMPS, 8 * PLANES, LANES), F32),
            pltpu.SemaphoreType.DMA((COMPS,)),
        ],
        compiler_params=pltpu.CompilerParams(vmem_limit_bytes=LIMIT),
    )(kept, coeffs, source, right_sent, left_sent, right_got, left_got, restrict, prolong)
    corrected = corrected.reshape(COMPS, 2, TILES, 8, LANES)
    fix = fix.reshape(COMPS, BLOCKS, HALF, LANES)
    return (
        jnp.swapaxes(corrected, 2, 3).reshape(velocity.shape),
        jnp.swapaxes(fix, 1, 2).reshape(COMPS, HALF, COARSE),
    )


def solution(mesh):
    return jax.shard_map(
        shards,
        mesh=mesh,
        in_specs=(
            P(None, ("grp", "sub"), None),
            P(None, ("grp", "sub"), None),
            P(("grp", "sub"), None),
            P(("grp", "sub"), None),
        ),
        out_specs=(P(None, ("grp", "sub"), None), P(None, ("grp", "sub"), None)),
        check_vma=False,
    )
```

time: 28.5 us -> 23.8 us (0.84)
  local copies, waits for them, and re-layouts: 3.97 us -> 0 us
  waiting for transfers between devices: 2.73 us -> 2.35 us
    unnamed x8 -> x0, local copies, waits for them, and re-layouts: 3.97 us -> none
    ppermute x2, waiting for transfers between devices: 2.73 us -> 2.35 us  [the longest x1 1.71 us: shards(): left_got = lax.ppermute(left_sent, axes, [(j, i) for i, j in forward])]
  transfers between devices with their start and end apart: 2 -> 2, of which waited for: 1 -> 2; matrix products, arithmetic and copies ran while one was open for 0% -> 0% of each run, Pallas kernels for 0% -> 0%
where the time goes in v2:
time: 23.8 us; the launch traced here: 23.6 us
  starting transfers between devices  15.3 us (64%)
  Pallas kernels  5.33 us (22%)
  waiting for transfers between devices  2.35 us (10%)
  between operations  0.66 us (3%)
    ppermute x1, starting transfers between devices, shards(): left_got = lax.ppermute(left_sent, axes, [(j, i) for i, j in forward])  11 us
    ppermute x1, starting transfers between devices, shards(): right_got = lax.ppermute(right_sent, axes, forward)  4.28 us
    pallas_call x1, Pallas kernels, shards(): pl.pallas_call(local_kernel, out_shape=(message, message, coarse, fine, j...  2.76 us
    pallas_call x1, Pallas kernels, shards(): pl.pallas_call(finish_kernel, out_shape=(fine, coarse), in_specs=[VMEM] *...  2.57 us
    ppermute x1, waiting for transfers between devices, shards(): left_got = lax.ppermute(left_sent, axes, [(j, i) for i, j in forward])  1.71 us
    ppermute x1, waiting for transfers between devices, shards(): right_got = lax.ppermute(right_sent, axes, forward)  0.64 us
  transfers between devices with their start and end apart: 2, of which 2 were waited for; matrix products, arithmetic and copies ran while one was open for 0% of the time, Pallas kernels for 0%

profile of v2, /device:TPU:56, one launch (start us, length us, event | category | flops | bytes accessed | tf_op | source)
XLA Modules:
  0.0 23.6 jit_solution(5566864012175496701)
XLA Ops:
  0.6 2.8 %shard_map.59 = (f32[7,8,512]{2,1,0:T(8,128)S(1)}, f32[7,8,512]{2,1,0:T(8,128)S(1)}, f32[3,64,128]{2,1,0:T(8,128)S(1)}, f32[3,2,256,128]{3,2,1,0:T(8,128)S(1)}, ...) custom-call(f32[3,2,256,128]{3,2,1,0:T(8,128)} %bitcast.30, ...), custom_call_target="tpu_custom_call" | custom-call | tf_op jit(solution)/shard_map/pallas_call | solution.py:302
  3.4 4.3 %collective-permute-start = (f32[7,8,512]{2,1,0:T(8,128)S(1)}, f32[7,8,512]{2,1,0:T(8,128)S(1)}, u32[]{:S(2)}, u32[]{:S(2)}) collective-permute-start(f32[7,8,512]{2,1,0:T(8,128)S(1)} %get-tuple-element.14.right_sent), channel_id=1, source_target_pairs={{0,1},{1,2},{2,3},{3,4},{4,5},{5,6},{6,7},{7,8},{8,9},{9,10},{10,1... | collective-permute-start | bytes 344072 | tf_op jit(solution)/shard_map/ppermute | solution.py:327
  7.7 11.0 %collective-permute-start.1 = (f32[7,8,512]{2,1,0:T(8,128)S(1)}, f32[7,8,512]{2,1,0:T(8,128)S(1)}, u32[]{:S(2)}, u32[]{:S(2)}) collective-permute-start(f32[7,8,512]{2,1,0:T(8,128)S(1)} %get-tuple-element.15.left_sent), channel_id=1, source_target_pairs={{1,0},{2,1},{3,2},{4,3},{5,4},{6,5},{7,6},{8,7},{9,8},{10,9},{11,1... | collective-permute-start | bytes 344072 | tf_op jit(solution)/shard_map/ppermute | solution.py:328
  18.7 0.6 %collective-permute-done.right_got = f32[7,8,512]{2,1,0:T(8,128)S(1)} collective-permute-done((f32[7,8,512]{2,1,0:T(8,128)S(1)}, f32[7,8,512]{2,1,0:T(8,128)S(1)}, u32[]{:S(2)}, u32[]{:S(2)}) %collective-permute-start) | collective-permute-done | bytes 114720 | tf_op jit(solution)/shard_map/ppermute | solution.py:327
  19.3 1.7 %collective-permute-done.1.left_got = f32[7,8,512]{2,1,0:T(8,128)S(1)} collective-permute-done((f32[7,8,512]{2,1,0:T(8,128)S(1)}, f32[7,8,512]{2,1,0:T(8,128)S(1)}, u32[]{:S(2)}, u32[]{:S(2)}) %collective-permute-start.1) | collective-permute-done | bytes 114720 | tf_op jit(solution)/shard_map/ppermute | solution.py:328
  21.0 2.6 %shard_map.60 = (f32[3,2,256,128]{3,2,1,0:T(8,128)}, f32[3,64,128]{2,1,0:T(8,128)}) custom-call(f32[3,2,256,128]{3,2,1,0:T(8,128)S(1)} %get-tuple-element.11.v_ref, f32[64,128]{1,0:T(8,128)S(1)} %get-tuple-element.12.cv_ref, f32[3,64,128]{2,1,0:T(8,128)S(1)} %get-tuple-element.13.src_ref, f32[7,8,512]{2,1,0:T(8,128)S(1)} %get-tuple-element.14.right_sent, ...), custom_call_target="tpu_custom_call" | custom-call | tf_op jit(solution)/shard_map/pallas_call | solution.py:330
Async XLA Ops:
  3.4 15.9 %collective-permute-start = (f32[7,8,512]{2,1,0:T(8,128)S(1)}, f32[7,8,512]{2,1,0:T(8,128)S(1)}, u32[]{:S(2)}, u32[]{:S(2)}) collective-permute-start(f32[7,8,512]{2,1,0:T(8,128)S(1)} %get-tuple-element.14.right_sent), channel_id=1, source_target_pairs={{0,1},{1,2},{2,3},{3,4},{4,5},{5,6},{6,7},{7,8},{8,9},{9,10},{10,1... | collective-permute-start | bytes 344072 | tf_op jit(solution)/shard_map/ppermute | solution.py:327
  7.7 13.4 %collective-permute-start.1 = (f32[7,8,512]{2,1,0:T(8,128)S(1)}, f32[7,8,512]{2,1,0:T(8,128)S(1)}, u32[]{:S(2)}, u32[]{:S(2)}) collective-permute-start(f32[7,8,512]{2,1,0:T(8,128)S(1)} %get-tuple-element.15.left_sent), channel_id=1, source_target_pairs={{1,0},{2,1},{3,2},{4,3},{5,4},{6,5},{7,6},{8,7},{9,8},{10,9},{11,1... | collective-permute-start | bytes 344072 | tf_op jit(solution)/shard_map/ppermute | solution.py:328

commit v3 on v2

v3 whole, which is shorter than its diff:
```python
import jax
import jax.numpy as jnp
from jax import lax
from jax.experimental import pallas as pl
from jax.experimental.pallas import tpu as pltpu
from jax.sharding import PartitionSpec as P

NY = 32
NZ = 32
DEGREE = 3
LOWER_EIG = 0.15
UPPER_EIG = 1.95
CENTER = 0.5 * (UPPER_EIG + LOWER_EIG)
HALF_WIDTH = 0.5 * (UPPER_EIG - LOWER_EIG)

COMPS = 3
FINE = 4 * NY * NZ
COARSE = NY * NZ
PLANES = 16
HALF = PLANES // 2
LANES = 128
BLOCKS = COARSE // LANES
WIDE = FINE // BLOCKS
TILES = FINE // LANES
F32 = jnp.float32
BF16 = jnp.bfloat16


def tile(index):
    return slice(LANES * index, LANES * (index + 1))


def fill_restrict(ref):
    fine = lax.broadcasted_iota(jnp.int32, (2 * NZ, LANES), 0)
    lane = lax.broadcasted_iota(jnp.int32, (2 * NZ, LANES), 1)
    apart = (fine - 2 * (lane % NZ) + 2 * NZ) % (2 * NZ)
    cols = jnp.where(apart == 0, 1.0, jnp.where((apart == 1) | (apart == 2 * NZ - 1), 0.5, 0.0))
    for row in range(8):
        away = jnp.abs(2 * (lane // NZ) - row)
        rows = jnp.where(away == 0, 1.0, jnp.where(away == 1, 0.5, 0.0))
        at = slice(2 * NZ * row, 2 * NZ * (row + 1))
        ref[at, :LANES] = (cols * rows).astype(BF16)
        beyond = jnp.where(lane < NZ, 0.5 * cols, 0.0) if row == 7 else jnp.zeros_like(cols)
        ref[at, LANES:] = beyond.astype(BF16)


def fill_prolong(ref):
    coarse = lax.broadcasted_iota(jnp.int32, (NZ, LANES), 0)
    lane = lax.broadcasted_iota(jnp.int32, (NZ, LANES), 1)
    apart = (lane - 2 * coarse + 2 * NZ) % (2 * NZ)
    cols = jnp.where(apart == 0, 1.0, jnp.where((apart == 1) | (apart == 2 * NZ - 1), 0.5, 0.0))
    for row in range(8):
        for part in range(4):
            away = jnp.abs(2 * row - 2 * part - lane // (2 * NZ))
            rows = jnp.where(away == 0, 1.0, jnp.where(away == 1, 0.5, 0.0))
            kept = cols * rows if row < 5 else jnp.zeros_like(cols)
            ref[NZ * row : NZ * (row + 1), tile(part)] = kept.astype(BF16)


def split_dot(left, matrix):
    high = left.astype(BF16)
    low = (left - high.astype(F32)).astype(BF16)
    return jnp.dot(high, matrix, preferred_element_type=F32) + jnp.dot(
        low, matrix, preferred_element_type=F32
    )


def iotas(rows):
    row = lax.broadcasted_iota(jnp.int32, (rows, LANES), 0)
    lane = lax.broadcasted_iota(jnp.int32, (rows, LANES), 1)
    return row, lane


def eight(index):
    return slice(8 * index, 8 * (index + 1))


def place():
    at = lax.axis_index("sub")
    return at, lax.rem(at, 2), at < lax.axis_size("sub") - 2


def local_half(h, v_ref, f_ref, c_ref, w_ref, cross_ref, ready):
    row, lane = iotas(8)
    low_half = lane < 64
    first_col = lane % 64 == 0
    last_col = lane % 64 == 63
    upper = h == 1
    matrix = w_ref[...]
    for k in range(COMPS):
        ready(k)
        values = [v_ref[k, h, eight(t), :] for t in range(TILES)]
        swapped = [pltpu.roll(x, 64, 1) for x in values]
        blocks = []
        for s in range(BLOCKS):
            pieces = []
            for t in range(4 * s, 4 * s + 4):
                x, turned = values[t], swapped[t]
                edge = v_ref[k, 1 - h, pl.ds(8 * t + 7 * h, 1), :]
                beside = turned + jnp.where(low_half, swapped[t - 1], swapped[(t + 1) % TILES])
                beside += pltpu.roll(jnp.where(last_col, turned, x), 1, 1)
                beside += pltpu.roll(jnp.where(first_col, turned, x), LANES - 1, 1)
                beside += jnp.where(row == 0, jnp.where(upper, edge, 0.0), pltpu.roll(x, 1, 0))
                beside += jnp.where(row == 7, jnp.where(upper, 0.0, edge), pltpu.roll(x, 7, 0))
                coeff = c_ref[h, eight(t), :]
                pieces.append(f_ref[k, h, eight(t), :] - x + coeff * (beside - 6.0 * x))
            blocks.append(jnp.concatenate(pieces, axis=1))
        sums = split_dot(jnp.concatenate(blocks, axis=0), matrix)
        parts = [sums[eight(s)] for s in range(BLOCKS)]
        for s in range(BLOCKS):
            cross_ref[k, h, eight(s), :] = parts[s][:, :LANES] + parts[s - 1][:, LANES:]


def write_message(h, ref, v_ref, c_ref, cv_ref, cross_ref):
    upper = h == 1
    for part in range(4):
        rows = pl.ds(8 * part + 7 * h, 8, 32)
        ref[COMPS, :, tile(part)] = c_ref[h, rows, :]
        for k in range(COMPS):
            ref[k, :, tile(part)] = v_ref[k, h, rows, :]
    for j in range(3):
        ref[4 + j, :, tile(COMPS)] = cv_ref[pl.ds(j + h * min(6, 7 - j), 8, 8), :]
    for k in range(COMPS):
        planes = [cross_ref[k, h, pl.ds(i, 8, 8), :] for i in range(8)]

        def source(i):
            return 0.125 * planes[i] + 0.0625 * (planes[i - 1] + planes[i + 1])

        middle = source(4)
        first = 0.125 * planes[0] + 0.0625 * planes[1]
        ref[4, :, tile(k)] = jnp.where(upper, middle, first)
        ref[5, :, tile(k)] = jnp.where(upper, source(6), source(2))
        ref[6, :, tile(k)] = jnp.where(upper, 0.0625 * planes[7], middle)


def local_kernel(
    v_hbm,
    f_hbm,
    c_hbm,
    cv_hbm,
    early_ref,
    middle_ref,
    cross_ref,
    v_ref,
    f_ref,
    c_ref,
    cv_ref,
    w_ref,
    q_ref,
    sems,
):
    _, h, early = place()
    copies = [pltpu.make_async_copy(c_hbm.at[h], c_ref.at[h], sems.at[0])]
    for k in range(COMPS):
        copies.append(pltpu.make_async_copy(v_hbm.at[k], v_ref.at[k], sems.at[1 + 2 * k]))
        copies.append(pltpu.make_async_copy(f_hbm.at[k, h], f_ref.at[k, h], sems.at[2 + 2 * k]))
    copies.append(pltpu.make_async_copy(cv_hbm, cv_ref, sems.at[7]))
    copies.append(pltpu.make_async_copy(c_hbm.at[1 - h], c_ref.at[1 - h], sems.at[8]))
    for k in range(COMPS):
        copies.append(
            pltpu.make_async_copy(f_hbm.at[k, 1 - h], f_ref.at[k, 1 - h], sems.at[9 + k])
        )
    for copy in copies:
        copy.start()
    fill_restrict(w_ref)
    fill_prolong(q_ref)

    def ready(k):
        if k == 0:
            copies[0].wait()
        copies[1 + 2 * k].wait()
        copies[2 + 2 * k].wait()

    local_half(h, v_ref, f_ref, c_ref, w_ref, cross_ref, ready)
    for copy in copies[7:]:
        copy.wait()
    write_message(h, middle_ref, v_ref, c_ref, cv_ref, cross_ref)

    @pl.when(early)
    def _():
        local_half(1 - h, v_ref, f_ref, c_ref, w_ref, cross_ref, lambda k: None)
        write_message(1 - h, early_ref, v_ref, c_ref, cv_ref, cross_ref)


def late_kernel(
    after, early_in, cross_in, v_ref, f_ref, c_ref, cv_ref, w_ref, early_ref, cross_ref
):
    del after
    _, h, early = place()
    cross_ref[:, h] = cross_in[:, h]

    @pl.when(early)
    def _():
        early_ref[...] = early_in[...]
        cross_ref[:, 1 - h] = cross_in[:, 1 - h]

    @pl.when(jnp.logical_not(early))
    def _():
        local_half(1 - h, v_ref, f_ref, c_ref, w_ref, cross_ref, lambda k: None)
        write_message(1 - h, early_ref, v_ref, c_ref, cv_ref, cross_ref)


def finish_half(h, sent, got, cross_ref, v_ref, cv_ref, w_ref, q_ref, mix_vm, out_vm, out_hbm, sems, keep_fix):
    _, lane = iotas(8)
    kept_up = lane < LANES - NZ
    kept_down = lane >= NZ
    first_col = lane % NZ == 0
    last_col = lane % NZ == NZ - 1
    whole = slice(0, WIDE)

    their_coeff, own_coeff = got(COMPS, whole), sent(COMPS, whole)
    rows = [got(k, whole) * own_coeff for k in range(COMPS)]
    rows += [sent(k, whole) * their_coeff for k in range(COMPS)]
    sums = split_dot(jnp.concatenate(rows, axis=0), w_ref[...])
    terms = []
    for part in range(2 * COMPS):
        mine = sums[eight(part)]
        terms.append(mine[:, :LANES] + pltpu.roll(mine[:, LANES:], 1, 0))

    first = 4 * h - 2
    last = first + 8
    inverse, quotient = {}, {}
    for j in range(first, last + 1):
        if j < 0:
            coeff = got(6 + j, tile(COMPS))
        elif j < HALF:
            coeff = cv_ref[pl.ds(j, 8, 8), :]
        else:
            coeff = got(4 + j - HALF, tile(COMPS))
        if j == HALF:
            inside = coeff > 0.0
        inverse[j] = 1.0 / (1.0 + 6.0 * coeff)
        quotient[j] = coeff * inverse[j]

    def near_sum(planes, j):
        x = planes[j]
        up = pltpu.roll(x, LANES - NZ, 1)
        down = pltpu.roll(x, NZ, 1)
        total = planes[j - 1] + planes[j + 1]
        total += jnp.where(kept_up, up, pltpu.roll(up, 7, 0))
        total += jnp.where(kept_down, down, pltpu.roll(down, 1, 0))
        total += pltpu.roll(jnp.where(last_col, up, x), 1, 1)
        total += pltpu.roll(jnp.where(first_col, down, x), LANES - 1, 1)
        return total

    sigma = CENTER / HALF_WIDTH
    stores = []
    for k in range(COMPS):
        at = tile(k)
        theirs, ours = terms[k], terms[COMPS + k]

        def crossed(p):
            return cross_ref[k, p // 8, pl.ds(p % 8, 8, 8), :]

        source = {}
        for j in range(max(first, 0), min(last, HALF - 1) + 1):
            beside = crossed(2 * j + 1)
            if j > 0:
                beside += crossed(2 * j - 1)
            source[j] = 0.125 * crossed(2 * j) + 0.0625 * beside
        if h == 0:
            source[-2] = got(4, at)
            source[-1] = got(5, at) + 0.0625 * ours
            source[0] += got(6, at) + (0.125 * theirs + 0.0625 * ours)
        else:
            source[HALF - 1] += 0.0625 * theirs
            after = sent(6, at) + got(4, at) + (0.0625 * theirs + 0.125 * ours)
            source[HALF] = jnp.where(inside, after, 0.0)
            source[HALF + 1] = got(5, at)
            source[HALF + 2] = got(6, at)

        scaled = {j: source[j] * inverse[j] for j in source}
        update = {j: x * (1.0 / CENTER) for j, x in scaled.items()}
        approx = update
        ratio_old = 1.0 / sigma
        for sweep in range(1, DEGREE):
            ratio_new = 1.0 / (2.0 * sigma - ratio_old)
            keep, gain = ratio_new * ratio_old, 2.0 * ratio_new / HALF_WIDTH
            inner = range(first + sweep, last - sweep + 1)
            update = {
                j: keep * update[j]
                + gain * (scaled[j] - approx[j] + quotient[j] * near_sum(approx, j))
                for j in inner
            }
            approx = {j: approx[j] + update[j] for j in inner}
            ratio_old = ratio_new

        for i in range(4):
            here, after = approx[4 * h + i], approx[4 * h + i + 1]
            keep_fix(k, i, here)
            mix_vm[k, eight(2 * i), :] = here
            mix_vm[k, eight(2 * i + 1), :] = 0.5 * (here + after)
        mixed = [mix_vm[k, pl.ds(s, 8, 8), :] for s in range(BLOCKS)]
        left = [
            jnp.concatenate([mixed[s], mixed[(s + 1) % BLOCKS]], axis=1) for s in range(BLOCKS)
        ]
        fine = split_dot(jnp.concatenate(left, axis=0), q_ref[...])
        for t in range(TILES):
            add = fine[eight(t // 4), tile(t % 4)]
            out_vm[k, h, eight(t), :] = v_ref[k, h, eight(t), :] + add
        store = pltpu.make_async_copy(out_vm.at[k, h], out_hbm.at[k, h], sems.at[k, h])
        store.start()
        stores.append(store)
    return stores


def upper_kernel(
    early_in,
    middle_in,
    early_got,
    cross_ref,
    v_ref,
    cv_ref,
    w_ref,
    q_ref,
    middle_ref,
    out_hbm,
    fix_ref,
    mix_vm,
    out_vm,
    sems,
):
    del middle_in, middle_ref
    at, _, _ = place()

    @pl.when(at == 0)
    def _():
        def keep_fix(k, i, plane):
            fix_ref[k, eight(i), :] = plane

        stores = finish_half(
            1,
            lambda slab, lanes: early_in[slab, :, lanes],
            lambda slab, lanes: early_got[slab, :, lanes],
            cross_ref,
            v_ref,
            cv_ref,
            w_ref,
            q_ref,
            mix_vm,
            out_vm,
            out_hbm,
            sems,
            keep_fix,
        )
        for store in stores:
            store.wait()


def lower_kernel(
    out_in,
    upper_fix,
    middle_sent,
    middle_got,
    cross_ref,
    v_ref,
    cv_ref,
    w_ref,
    q_ref,
    out_hbm,
    fix_hbm,
    mix_vm,
    out_vm,
    sems,
    fix_vm,
    fix_sem,
):
    del out_in
    at, _, _ = place()

    @pl.when(at == 0)
    def _():
        def keep_fix(k, i, plane):
            fix_vm[k, pl.ds(i, 8, 8), :] = plane

        for k in range(COMPS):
            for i in range(4):
                fix_vm[k, pl.ds(4 + i, 8, 8), :] = upper_fix[k, eight(i), :]
        stores = finish_half(
            0,
            lambda slab, lanes: middle_sent[slab, :, lanes],
            lambda slab, lanes: middle_got[slab, :, lanes],
            cross_ref,
            v_ref,
            cv_ref,
            w_ref,
            q_ref,
            mix_vm,
            out_vm,
            out_hbm,
            sems,
            keep_fix,
        )
        fix_copy = pltpu.make_async_copy(fix_vm, fix_hbm, fix_sem)
        fix_copy.start()
        for store in stores:
            store.wait()
        fix_copy.wait()


def finish_kernel(
    out_in,
    fix_in,
    early_sent,
    middle_sent,
    middle_got,
    early_got,
    late_got,
    cross_ref,
    v_ref,
    cv_ref,
    w_ref,
    q_ref,
    out_hbm,
    fix_hbm,
    mix_vm,
    out_vm,
    sems,
    fix_vm,
    fix_sem,
):
    del out_in, fix_in
    at, h, early = place()
    even = h == 0

    def outer_got(slab, lanes):
        return jnp.where(early, early_got[slab, :, lanes], late_got[slab, :, lanes])

    def left_sent(slab, lanes):
        return jnp.where(even, middle_sent[slab, :, lanes], early_sent[slab, :, lanes])

    def left_got(slab, lanes):
        return jnp.where(even, middle_got[slab, :, lanes], outer_got(slab, lanes))

    def right_sent(slab, lanes):
        return jnp.where(even, early_sent[slab, :, lanes], middle_sent[slab, :, lanes])

    def right_got(slab, lanes):
        return jnp.where(even, outer_got(slab, lanes), middle_got[slab, :, lanes])

    def half(which, sent, got):
        def keep_fix(k, i, plane):
            fix_vm[k, pl.ds(4 * which + i, 8, 8), :] = plane

        refs = (cross_ref, v_ref, cv_ref, w_ref, q_ref, mix_vm, out_vm, out_hbm, sems, keep_fix)
        return finish_half(which, sent, got, *refs)

    @pl.when(at != 0)
    def _():
        stores = half(0, left_sent, left_got) + half(1, right_sent, right_got)
        fix_copy = pltpu.make_async_copy(fix_vm, fix_hbm, fix_sem)
        fix_copy.start()
        for store in stores:
            store.wait()
        fix_copy.wait()


VMEM = pl.BlockSpec(memory_space=pltpu.VMEM)
HBM = pl.BlockSpec(memory_space=pltpu.HBM)
ANY = pl.BlockSpec(memory_space=pl.ANY)
PARAMS = pltpu.CompilerParams(vmem_limit_bytes=16 * 2**20)
FINE_TILED = (2, 8 * TILES, LANES)


def fine_tiled(field):
    lead = field.shape[:-2]
    split = field.reshape(lead + (2, 8, TILES, LANES))
    return jnp.swapaxes(split, -3, -2).reshape(lead + FINE_TILED)


def pinned(field):
    return pltpu.with_memory_space_constraint(field, pltpu.HBM)


def shards(velocity, forcing, viscosity, coarse_visc):
    coeffs = jnp.swapaxes(coarse_visc.reshape(HALF, BLOCKS, LANES), 0, 1).reshape(8 * HALF, LANES)
    message = jax.ShapeDtypeStruct((7, 8, WIDE), F32)
    fine = jax.ShapeDtypeStruct((COMPS,) + FINE_TILED, F32)
    coarse = jax.ShapeDtypeStruct((COMPS, 8 * HALF, LANES), F32)
    crosses = jax.ShapeDtypeStruct((COMPS, 2, 8 * 8, LANES), F32)
    early, middle, cross, v_kept, f_kept, c_kept, cv_kept, restrict, prolong = pl.pallas_call(
        local_kernel,
        out_shape=(
            message,
            message,
            crosses,
            fine,
            fine,
            jax.ShapeDtypeStruct(FINE_TILED, F32),
            jax.ShapeDtypeStruct((8 * HALF, LANES), F32),
            jax.ShapeDtypeStruct((WIDE, 2 * LANES), BF16),
            jax.ShapeDtypeStruct((2 * LANES, WIDE), BF16),
        ),
        in_specs=[HBM] * 4,
        out_specs=(VMEM,) * 9,
        scratch_shapes=[pltpu.SemaphoreType.DMA((12,))],
        compiler_params=PARAMS,
    )(
        pinned(fine_tiled(velocity)),
        pinned(fine_tiled(forcing)),
        pinned(fine_tiled(viscosity)),
        pinned(coeffs),
    )

    axes = ("grp", "sub")
    count, deep = lax.axis_size(axes), lax.axis_size("sub")

    def swap(block, kept):
        pairs = [(i, i + 1) for i in range(count - 1) if kept(i)]
        return lax.ppermute(block, axes, pairs + [(j, i) for i, j in pairs])

    early_got = swap(early, lambda i: i % 2 == 0 and i % deep < deep - 2)
    half_scratch = [
        pltpu.VMEM((COMPS, 8 * 8, LANES), F32),
        pltpu.VMEM((COMPS,) + FINE_TILED, F32),
    ]
    middle, corrected, upper_fix = pl.pallas_call(
        upper_kernel,
        out_shape=(message, fine, jax.ShapeDtypeStruct((COMPS, 4 * 8, LANES), F32)),
        in_specs=[VMEM, ANY] + [VMEM] * 6,
        out_specs=(ANY, HBM, VMEM),
        input_output_aliases={1: 0},
        scratch_shapes=half_scratch + [pltpu.SemaphoreType.DMA((COMPS, 2))],
        compiler_params=PARAMS,
    )(early, middle, early_got, cross, v_kept, cv_kept, restrict, prolong)
    middle_got = swap(middle, lambda i: i % 2 == 1)
    cross_local = cross
    early, cross = pl.pallas_call(
        late_kernel,
        out_shape=(message, crosses),
        in_specs=[ANY] + [VMEM] * 7,
        out_specs=(VMEM, VMEM),
        compiler_params=PARAMS,
        cost_estimate=pl.CostEstimate(flops=10**9, bytes_accessed=10**7, transcendentals=0),
    )(upper_fix, early, cross, v_kept, f_kept, c_kept, cv_kept, restrict)
    late_got = swap(early, lambda i: i % 2 == 0 and i % deep == deep - 2)

    finish_scratch = half_scratch + [
        pltpu.SemaphoreType.DMA((COMPS, 2)),
        pltpu.VMEM((COMPS, 8 * HALF, LANES), F32),
        pltpu.SemaphoreType.DMA,
    ]
    kept = (v_kept, cv_kept, restrict, prolong)
    corrected, fix = pl.pallas_call(
        lower_kernel,
        out_shape=(fine, coarse),
        in_specs=[HBM] + [VMEM] * 8,
        out_specs=(HBM, HBM),
        input_output_aliases={0: 0},
        scratch_shapes=finish_scratch,
        compiler_params=PARAMS,
    )(pinned(corrected), upper_fix, middle, middle_got, cross_local, *kept)
    corrected, fix = pl.pallas_call(
        finish_kernel,
        out_shape=(fine, coarse),
        in_specs=[HBM, HBM] + [VMEM] * 10,
        out_specs=(HBM, HBM),
        input_output_aliases={0: 0, 1: 1},
        scratch_shapes=finish_scratch,
        compiler_params=PARAMS,
    )(pinned(corrected), pinned(fix), early, middle, middle_got, early_got, late_got, cross, *kept)
    corrected = corrected.reshape(COMPS, 2, TILES, 8, LANES)
    fix = fix.reshape(COMPS, BLOCKS, HALF, LANES)
    return (
        jnp.swapaxes(corrected, 2, 3).reshape(velocity.shape),
        jnp.swapaxes(fix, 1, 2).reshape(COMPS, HALF, COARSE),
    )


def solution(mesh):
    return jax.shard_map(
        shards,
        mesh=mesh,
        in_specs=(
            P(None, ("grp", "sub"), None),
            P(None, ("grp", "sub"), None),
            P(("grp", "sub"), None),
            P(("grp", "sub"), None),
        ),
        out_specs=(P(None, ("grp", "sub"), None), P(None, ("grp", "sub"), None)),
        check_vma=False,
    )
```

time: 23.8 us -> 26.5 us (1.11)
  the two profiles are of different devices: /device:TPU:56 before, /device:TPU:32 now
where the time goes in v3:
time: 26.5 us; the launch traced here: 26.4 us
  waiting for transfers between devices  10.6 us (40%)
  starting transfers between devices  8.27 us (31%)
  Pallas kernels  6.8 us (26%)
  between operations  0.69 us (3%)
    ppermute x3, waiting for transfers between devices, swap(): return lax.ppermute(block, axes, pairs + [(j, i) for i, j in pairs])  10.6 us
    ppermute x3, starting transfers between devices, swap(): return lax.ppermute(block, axes, pairs + [(j, i) for i, j in pairs])  8.27 us
    pallas_call x1, Pallas kernels, shards(): pl.pallas_call(local_kernel, out_shape=(message, message, crosses, fine,...  3.04 us
    pallas_call x1, Pallas kernels, shards(): pl.pallas_call(lower_kernel, out_shape=(fine, coarse), in_specs=[HBM] + [...  1.83 us
    pallas_call x1, Pallas kernels, shards(): pl.pallas_call(upper_kernel, out_shape=(message, fine, jax.ShapeDtypeStru...  1.81 us
  transfers between devices with their start and end apart: 3, of which 2 were waited for; matrix products, arithmetic and copies ran while one was open for 0% of the time, Pallas kernels for 7%

profile of v3, /device:TPU:32, one launch (start us, length us, event | category | flops | bytes accessed | tf_op | source)
XLA Modules:
  0.0 26.4 jit_solution(3818477411661181610)
XLA Ops:
  0.6 3.0 %shard_map.59 = (f32[7,8,512]{2,1,0:T(8,128)S(1)}, f32[7,8,512]{2,1,0:T(8,128)S(1)}, f32[3,2,64,128]{3,2,1,0:T(8,128)S(1)}, f32[3,2,256,128]{3,2,1,0:T(8,128)S(1...) custom-call(f32[3,2,256,128]{3,2,1,0:T(8,128)} %bitcast.31, ...), custom_call_target="tpu_custom_call" | custom-call | tf_op jit(solution)/shard_map/pallas_call | solution.py:481
  3.7 4.3 %collective-permute-start = (f32[7,8,512]{2,1,0:T(8,128)S(1)}, f32[7,8,512]{2,1,0:T(8,128)S(1)}, u32[]{:S(2)}, u32[]{:S(2)}) collective-permute-start(f32[7,8,512]{2,1,0:T(8,128)S(1)} %get-tuple-element.20.early_in), channel_id=1, source_target_pairs={{0,1},{2,3},{4,5},{8,9},{10,11},{12,13},{16,17},{18,19},{20,21},{2... | collective-permute-start | bytes 344072 | tf_op jit(solution)/shard_map/ppermute | solution.py:510
  8.0 3.1 %collective-permute-done.early_got = f32[7,8,512]{2,1,0:T(8,128)S(1)} collective-permute-done((f32[7,8,512]{2,1,0:T(8,128)S(1)}, f32[7,8,512]{2,1,0:T(8,128)S(1)}, u32[]{:S(2)}, u32[]{:S(2)}) %collective-permute-start) | collective-permute-done | bytes 114720 | tf_op jit(solution)/shard_map/ppermute | solution.py:510
  11.1 1.8 %shard_map.60 = (f32[7,8,512]{2,1,0:T(8,128)S(1)}, f32[3,2,256,128]{3,2,1,0:T(8,128)}, f32[3,32,128]{2,1,0:T(8,128)S(1)}) custom-call(f32[7,8,512]{2,1,0:T(8,128)S(1)} %get-tuple-element.20.early_in, f32[7,8,512]{2,1,0:T(8,128)S(1)} %get-tuple-element.21.middle_in, f32[7,8,512]{2,1,0:T(8,128)S(1)} %collective-permute-done.early_got, ...), custom_call_target="tpu_custom_call", output_to_operand_aliasing={{0}: (1, {})} | custom-call | tf_op jit(solution)/shard_map/pallas_call | solution.py:517
  12.9 3.3 %collective-permute-start.1 = (f32[7,8,512]{2,1,0:T(8,128)S(1)}, f32[7,8,512]{2,1,0:T(8,128)S(1)}, u32[]{:S(2)}, u32[]{:S(2)}) collective-permute-start(f32[7,8,512]{2,1,0:T(8,128)S(1)} %get-tuple-element.29.middle_sent), channel_id=1, source_target_pairs={{1,2},{3,4},{5,6},{7,8},{9,10},{11,12},{13,14},{15,16},{17,18},{19... | collective-permute-start | bytes 344072 | tf_op jit(solution)/shard_map/ppermute | solution.py:510
  16.3 0.7 %collective-permute-start.2 = (f32[7,8,512]{2,1,0:T(8,128)S(1)}, f32[7,8,512]{2,1,0:T(8,128)S(1)}, u32[]{:S(2)}, u32[]{:S(2)}) collective-permute-start(f32[7,8,512]{2,1,0:T(8,128)S(1)} %get-tuple-element.34.early_sent), channel_id=1, source_target_pairs={{6,7},{14,15},{22,23},{30,31},{38,39},{46,47},{54,55},{62,63},{70,... | collective-permute-start | bytes 344072 | tf_op jit(solution)/shard_map/ppermute | solution.py:510
  17.0 7.5 %collective-permute-done.1.middle_got = f32[7,8,512]{2,1,0:T(8,128)S(1)} collective-permute-done((f32[7,8,512]{2,1,0:T(8,128)S(1)}, f32[7,8,512]{2,1,0:T(8,128)S(1)}, u32[]{:S(2)}, u32[]{:S(2)}) %collective-permute-start.1) | collective-permute-done | bytes 114720 | tf_op jit(solution)/shard_map/ppermute | solution.py:510
  24.5 1.8 %shard_map.61 = (f32[3,2,256,128]{3,2,1,0:T(8,128)}, f32[3,64,128]{2,1,0:T(8,128)}) custom-call(f32[3,2,256,128]{3,2,1,0:T(8,128)} %get-tuple-element.27.out_in, f32[3,32,128]{2,1,0:T(8,128)S(1)} %get-tuple-element.28.upper_fix.after, f32[7,8,512]{2,1,0:T(8,128)S(1)} %get-tuple-element.29.middle_sent, ...), custom_call_target="tpu_custom_call", output_to_operand_aliasing={{0}: (0, {})} | custom-call | tf_op jit(solution)/shard_map/pallas_call | solution.py:544
  26.3 0.0 collective-permute-done.2.late_got
  26.3 0.1 shard_map.63
  (1 shorter events, 0.0 us)
Async XLA Ops:
  3.7 7.4 %collective-permute-start = (f32[7,8,512]{2,1,0:T(8,128)S(1)}, f32[7,8,512]{2,1,0:T(8,128)S(1)}, u32[]{:S(2)}, u32[]{:S(2)}) collective-permute-start(f32[7,8,512]{2,1,0:T(8,128)S(1)} %get-tuple-element.20.early_in), channel_id=1, source_target_pairs={{0,1},{2,3},{4,5},{8,9},{10,11},{12,13},{16,17},{18,19},{20,21},{2... | collective-permute-start | bytes 344072 | tf_op jit(solution)/shard_map/ppermute | solution.py:510
  12.9 11.5 %collective-permute-start.1 = (f32[7,8,512]{2,1,0:T(8,128)S(1)}, f32[7,8,512]{2,1,0:T(8,128)S(1)}, u32[]{:S(2)}, u32[]{:S(2)}) collective-permute-start(f32[7,8,512]{2,1,0:T(8,128)S(1)} %get-tuple-element.29.middle_sent), channel_id=1, source_target_pairs={{1,2},{3,4},{5,6},{7,8},{9,10},{11,12},{13,14},{15,16},{17,18},{19... | collective-permute-start | bytes 344072 | tf_op jit(solution)/shard_map/ppermute | solution.py:510
  16.3 10.0 %collective-permute-start.2 = (f32[7,8,512]{2,1,0:T(8,128)S(1)}, f32[7,8,512]{2,1,0:T(8,128)S(1)}, u32[]{:S(2)}, u32[]{:S(2)}) collective-permute-start(f32[7,8,512]{2,1,0:T(8,128)S(1)} %get-tuple-element.34.early_sent), channel_id=1, source_target_pairs={{6,7},{14,15},{22,23},{30,31},{38,39},{46,47},{54,55},{62,63},{70,... | collective-permute-start | bytes 344072 | tf_op jit(solution)/shard_map/ppermute | solution.py:510

commit v4 on v3

--- a/solution.py
+++ b/solution.py
@@ -75,129 +75,91 @@
     return slice(8 * index, 8 * (index + 1))
 
 
-def place():
-    at = lax.axis_index("sub")
-    return at, lax.rem(at, 2), at < lax.axis_size("sub") - 2
-
-
-def local_half(h, v_ref, f_ref, c_ref, w_ref, cross_ref, ready):
-    row, lane = iotas(8)
+def local_kernel(
+    v_hbm,
+    f_hbm,
+    c_hbm,
+    cv_hbm,
+    right_ref,
+    left_ref,
+    cross_ref,
+    v_ref,
+    cv_ref,
+    w_ref,
+    q_ref,
+    f_vm,
+    c_vm,
+    sems,
+):
+    copies = [pltpu.make_async_copy(c_hbm, c_vm, sems.at[0])]
+    for k in range(COMPS):
+        copies.append(pltpu.make_async_copy(v_hbm.at[k], v_ref.at[k], sems.at[1 + 2 * k]))
+        copies.append(pltpu.make_async_copy(f_hbm.at[k], f_vm.at[k], sems.at[2 + 2 * k]))
+    copies.append(pltpu.make_async_copy(cv_hbm, cv_ref, sems.at[1 + 2 * COMPS]))
+    for copy in copies:
+        copy.start()
+
+    row, lane = iotas(PLANES)
     low_half = lane < 64
     first_col = lane % 64 == 0
     last_col = lane % 64 == 63
-    upper = h == 1
+    fill_restrict(w_ref)
+    fill_prolong(q_ref)
     matrix = w_ref[...]
+
+    def packed_planes(slab, source):
+        for part in range(4):
+            left_ref[slab, :, tile(part)] = source[0, pl.ds(8 * part, 8, 32), :]
+            right_ref[slab, :, tile(part)] = source[1, pl.ds(8 * part + 7, 8, 32), :]
+
+    copies[0].wait()
+    packed_planes(COMPS, c_vm)
+
     for k in range(COMPS):
-        ready(k)
-        values = [v_ref[k, h, eight(t), :] for t in range(TILES)]
+        copies[1 + 2 * k].wait()
+        copies[2 + 2 * k].wait()
+
+        def planes_of(ref, t):
+            return jnp.concatenate([ref[0, eight(t), :], ref[1, eight(t), :]], axis=0)
+
+        values = [planes_of(v_ref.at[k], t) for t in range(TILES)]
         swapped = [pltpu.roll(x, 64, 1) for x in values]
         blocks = []
         for s in range(BLOCKS):
             pieces = []
             for t in range(4 * s, 4 * s + 4):
                 x, turned = values[t], swapped[t]
-                edge = v_ref[k, 1 - h, pl.ds(8 * t + 7 * h, 1), :]
                 beside = turned + jnp.where(low_half, swapped[t - 1], swapped[(t + 1) % TILES])
                 beside += pltpu.roll(jnp.where(last_col, turned, x), 1, 1)
                 beside += pltpu.roll(jnp.where(first_col, turned, x), LANES - 1, 1)
-                beside += jnp.where(row == 0, jnp.where(upper, edge, 0.0), pltpu.roll(x, 1, 0))
-                beside += jnp.where(row == 7, jnp.where(upper, 0.0, edge), pltpu.roll(x, 7, 0))
-                coeff = c_ref[h, eight(t), :]
-                pieces.append(f_ref[k, h, eight(t), :] - x + coeff * (beside - 6.0 * x))
+                beside += jnp.where(row == 0, 0.0, pltpu.roll(x, 1, 0))
+                beside += jnp.where(row == PLANES - 1, 0.0, pltpu.roll(x, PLANES - 1, 0))
+                pieces.append(
+                    planes_of(f_vm.at[k], t) - x + planes_of(c_vm, t) * (beside - 6.0 * x)
+                )
             blocks.append(jnp.concatenate(pieces, axis=1))
         sums = split_dot(jnp.concatenate(blocks, axis=0), matrix)
-        parts = [sums[eight(s)] for s in range(BLOCKS)]
+        parts = [sums[PLANES * s : PLANES * (s + 1)] for s in range(BLOCKS)]
         for s in range(BLOCKS):
-            cross_ref[k, h, eight(s), :] = parts[s][:, :LANES] + parts[s - 1][:, LANES:]
-
-
-def write_message(h, ref, v_ref, c_ref, cv_ref, cross_ref):
-    upper = h == 1
-    for part in range(4):
-        rows = pl.ds(8 * part + 7 * h, 8, 32)
-        ref[COMPS, :, tile(part)] = c_ref[h, rows, :]
-        for k in range(COMPS):
-            ref[k, :, tile(part)] = v_ref[k, h, rows, :]
+            crossed = parts[s][:, :LANES] + parts[s - 1][:, LANES:]
+            cross_ref[k, PLANES * s : PLANES * (s + 1), :] = crossed
+        planes = [cross_ref[k, pl.ds(p, 8, PLANES), :] for p in range(PLANES)]
+        half_odds = [0.0625 * planes[2 * j + 1] for j in range(HALF)]
+        sources = []
+        for j in range(HALF):
+            source = 0.125 * planes[2 * j] + half_odds[j]
+            if j > 0:
+                source += half_odds[j - 1]
+            sources.append(source)
+        for j in range(3):
+            left_ref[4 + j, :, tile(k)] = sources[j]
+            right_ref[4 + j, :, tile(k)] = (sources[6:] + half_odds[-1:])[j]
+        packed_planes(k, v_ref.at[k])
+
+    copies[-1].wait()
     for j in range(3):
-        ref[4 + j, :, tile(COMPS)] = cv_ref[pl.ds(j + h * min(6, 7 - j), 8, 8), :]
-    for k in range(COMPS):
-        planes = [cross_ref[k, h, pl.ds(i, 8, 8), :] for i in range(8)]
-
-        def source(i):
-            return 0.125 * planes[i] + 0.0625 * (planes[i - 1] + planes[i + 1])
-
-        middle = source(4)
-        first = 0.125 * planes[0] + 0.0625 * planes[1]
-        ref[4, :, tile(k)] = jnp.where(upper, middle, first)
-        ref[5, :, tile(k)] = jnp.where(upper, source(6), source(2))
-        ref[6, :, tile(k)] = jnp.where(upper, 0.0625 * planes[7], middle)
-
-
-def local_kernel(
-    v_hbm,
-    f_hbm,
-    c_hbm,
-    cv_hbm,
-    early_ref,
-    middle_ref,
-    cross_ref,
-    v_ref,
-    f_ref,
-    c_ref,
-    cv_ref,
-    w_ref,
-    q_ref,
-    sems,
-):
-    _, h, early = place()
-    copies = [pltpu.make_async_copy(c_hbm.at[h], c_ref.at[h], sems.at[0])]
-    for k in range(COMPS):
-        copies.append(pltpu.make_async_copy(v_hbm.at[k], v_ref.at[k], sems.at[1 + 2 * k]))
-        copies.append(pltpu.make_async_copy(f_hbm.at[k, h], f_ref.at[k, h], sems.at[2 + 2 * k]))
-    copies.append(pltpu.make_async_copy(cv_hbm, cv_ref, sems.at[7]))
-    copies.append(pltpu.make_async_copy(c_hbm.at[1 - h], c_ref.at[1 - h], sems.at[8]))
-    for k in range(COMPS):
-        copies.append(
-            pltpu.make_async_copy(f_hbm.at[k, 1 - h], f_ref.at[k, 1 - h], sems.at[9 + k])
-        )
-    for copy in copies:
-        copy.start()
-    fill_restrict(w_ref)
-    fill_prolong(q_ref)
-
-    def ready(k):
-        if k == 0:
-            copies[0].wait()
-        copies[1 + 2 * k].wait()
-        copies[2 + 2 * k].wait()
-
-    local_half(h, v_ref, f_ref, c_ref, w_ref, cross_ref, ready)
-    for copy in copies[7:]:
-        copy.wait()
-    write_message(h, middle_ref, v_ref, c_ref, cv_ref, cross_ref)
-
-    @pl.when(early)
-    def _():
-        local_half(1 - h, v_ref, f_ref, c_ref, w_ref, cross_ref, lambda k: None)
-        write_message(1 - h, early_ref, v_ref, c_ref, cv_ref, cross_ref)
-
-
-def late_kernel(
-    after, early_in, cross_in, v_ref, f_ref, c_ref, cv_ref, w_ref, early_ref, cross_ref
-):
-    del after
-    _, h, early = place()
-    cross_ref[:, h] = cross_in[:, h]
-
-    @pl.when(early)
-    def _():
-        early_ref[...] = early_in[...]
-        cross_ref[:, 1 - h] = cross_in[:, 1 - h]
-
-    @pl.when(jnp.logical_not(early))
-    def _():
-        local_half(1 - h, v_ref, f_ref, c_ref, w_ref, cross_ref, lambda k: None)
-        write_message(1 - h, early_ref, v_ref, c_ref, cv_ref, cross_ref)
+        left_ref[4 + j, :, tile(COMPS)] = cv_ref[pl.ds(j, 8, 8), :]
+        right_ref[4 + j, :, tile(COMPS)] = cv_ref[pl.ds(min(6 + j, 7), 8, 8), :]
 
 
 def finish_half(h, sent, got, cross_ref, v_ref, cv_ref, w_ref, q_ref, mix_vm, out_vm, out_hbm, sems, keep_fix):
@@ -250,7 +212,7 @@
         theirs, ours = terms[k], terms[COMPS + k]
 
         def crossed(p):
-            return cross_ref[k, p // 8, pl.ds(p % 8, 8, 8), :]
+            return cross_ref[k, pl.ds(p, 8, PLANES), :]
 
         source = {}
         for j in range(max(first, 0), min(last, HALF - 1) + 1):
@@ -305,33 +267,32 @@
 
 
 def upper_kernel(
-    early_in,
-    middle_in,
-    early_got,
+    left_in,
+    right_sent,
+    inner_got,
     cross_ref,
     v_ref,
     cv_ref,
     w_ref,
     q_ref,
-    middle_ref,
+    left_ref,
     out_hbm,
     fix_ref,
     mix_vm,
     out_vm,
     sems,
 ):
-    del middle_in, middle_ref
-    at, _, _ = place()
-
-    @pl.when(at == 0)
+    del left_in, left_ref
+
+    @pl.when(lax.axis_index("sub") == 0)
     def _():
         def keep_fix(k, i, plane):
             fix_ref[k, eight(i), :] = plane
 
         stores = finish_half(
             1,
-            lambda slab, lanes: early_in[slab, :, lanes],
-            lambda slab, lanes: early_got[slab, :, lanes],
+            lambda slab, lanes: right_sent[slab, :, lanes],
+            lambda slab, lanes: inner_got[slab, :, lanes],
             cross_ref,
             v_ref,
             cv_ref,
@@ -350,8 +311,8 @@
 def lower_kernel(
     out_in,
     upper_fix,
-    middle_sent,
-    middle_got,
+    left_sent,
+    right_got,
     cross_ref,
     v_ref,
     cv_ref,
@@ -366,9 +327,8 @@
     fix_sem,
 ):
     del out_in
-    at, _, _ = place()
-
-    @pl.when(at == 0)
+
+    @pl.when(lax.axis_index("sub") == 0)
     def _():
         def keep_fix(k, i, plane):
             fix_vm[k, pl.ds(i, 8, 8), :] = plane
@@ -378,8 +338,8 @@
                 fix_vm[k, pl.ds(4 + i, 8, 8), :] = upper_fix[k, eight(i), :]
         stores = finish_half(
             0,
-            lambda slab, lanes: middle_sent[slab, :, lanes],
-            lambda slab, lanes: middle_got[slab, :, lanes],
+            lambda slab, lanes: left_sent[slab, :, lanes],
+            lambda slab, lanes: right_got[slab, :, lanes],
             cross_ref,
             v_ref,
             cv_ref,
@@ -401,11 +361,11 @@
 def finish_kernel(
     out_in,
     fix_in,
-    early_sent,
-    middle_sent,
-    middle_got,
-    early_got,
-    late_got,
+    left_sent,
+    right_sent,
+    right_got,
+    inner_got,
+    outer_got,
     cross_ref,
     v_ref,
     cv_ref,
@@ -420,34 +380,23 @@
     fix_sem,
 ):
     del out_in, fix_in
-    at, h, early = place()
-    even = h == 0
-
-    def outer_got(slab, lanes):
-        return jnp.where(early, early_got[slab, :, lanes], late_got[slab, :, lanes])
-
-    def left_sent(slab, lanes):
-        return jnp.where(even, middle_sent[slab, :, lanes], early_sent[slab, :, lanes])
+    at = lax.axis_index("sub")
+    inner = at < lax.axis_size("sub") - 2
 
     def left_got(slab, lanes):
-        return jnp.where(even, middle_got[slab, :, lanes], outer_got(slab, lanes))
-
-    def right_sent(slab, lanes):
-        return jnp.where(even, early_sent[slab, :, lanes], middle_sent[slab, :, lanes])
-
-    def right_got(slab, lanes):
-        return jnp.where(even, outer_got(slab, lanes), middle_got[slab, :, lanes])
+        return jnp.where(inner, inner_got[slab, :, lanes], outer_got[slab, :, lanes])
 
     def half(which, sent, got):
         def keep_fix(k, i, plane):
             fix_vm[k, pl.ds(4 * which + i, 8, 8), :] = plane
 
         refs = (cross_ref, v_ref, cv_ref, w_ref, q_ref, mix_vm, out_vm, out_hbm, sems, keep_fix)
-        return finish_half(which, sent, got, *refs)
+        return finish_half(which, lambda slab, lanes: sent[slab, :, lanes], got, *refs)
 
     @pl.when(at != 0)
     def _():
-        stores = half(0, left_sent, left_got) + half(1, right_sent, right_got)
+        stores = half(0, left_sent, lambda slab, lanes: right_got[slab, :, lanes])
+        stores += half(1, right_sent, left_got)
         fix_copy = pltpu.make_async_copy(fix_vm, fix_hbm, fix_sem)
         fix_copy.start()
         for store in stores:
@@ -477,23 +426,25 @@
     message = jax.ShapeDtypeStruct((7, 8, WIDE), F32)
     fine = jax.ShapeDtypeStruct((COMPS,) + FINE_TILED, F32)
     coarse = jax.ShapeDtypeStruct((COMPS, 8 * HALF, LANES), F32)
-    crosses = jax.ShapeDtypeStruct((COMPS, 2, 8 * 8, LANES), F32)
-    early, middle, cross, v_kept, f_kept, c_kept, cv_kept, restrict, prolong = pl.pallas_call(
+    crosses = jax.ShapeDtypeStruct((COMPS, 8 * PLANES, LANES), F32)
+    right_sent, left_sent, cross, *kept = pl.pallas_call(
         local_kernel,
         out_shape=(
             message,
             message,
             crosses,
             fine,
-            fine,
-            jax.ShapeDtypeStruct(FINE_TILED, F32),
             jax.ShapeDtypeStruct((8 * HALF, LANES), F32),
             jax.ShapeDtypeStruct((WIDE, 2 * LANES), BF16),
             jax.ShapeDtypeStruct((2 * LANES, WIDE), BF16),
         ),
         in_specs=[HBM] * 4,
-        out_specs=(VMEM,) * 9,
-        scratch_shapes=[pltpu.SemaphoreType.DMA((12,))],
+        out_specs=(VMEM,) * 7,
+        scratch_shapes=[
+            pltpu.VMEM((COMPS,) + FINE_TILED, F32),
+            pltpu.VMEM(FINE_TILED, F32),
+            pltpu.SemaphoreType.DMA((2 + 2 * COMPS,)),
+        ],
         compiler_params=PARAMS,
     )(
         pinned(fine_tiled(velocity)),
@@ -504,43 +455,29 @@
 
     axes = ("grp", "sub")
     count, deep = lax.axis_size(axes), lax.axis_size("sub")
-
-    def swap(block, kept):
-        pairs = [(i, i + 1) for i in range(count - 1) if kept(i)]
-        return lax.ppermute(block, axes, pairs + [(j, i) for i, j in pairs])
-
-    early_got = swap(early, lambda i: i % 2 == 0 and i % deep < deep - 2)
+    inner = [(i + 1, i) for i in range(count - 1) if i % deep < deep - 2]
+    outer = [(i + 1, i) for i in range(count - 1) if i % deep >= deep - 2]
+    right_got = lax.ppermute(right_sent, axes, [(i, i + 1) for i in range(count - 1)])
+    inner_got = lax.ppermute(left_sent, axes, inner)
     half_scratch = [
         pltpu.VMEM((COMPS, 8 * 8, LANES), F32),
         pltpu.VMEM((COMPS,) + FINE_TILED, F32),
     ]
-    middle, corrected, upper_fix = pl.pallas_call(
+    left_sent, corrected, upper_fix = pl.pallas_call(
         upper_kernel,
         out_shape=(message, fine, jax.ShapeDtypeStruct((COMPS, 4 * 8, LANES), F32)),
-        in_specs=[VMEM, ANY] + [VMEM] * 6,
+        in_specs=[ANY] + [VMEM] * 7,
         out_specs=(ANY, HBM, VMEM),
-        input_output_aliases={1: 0},
+        input_output_aliases={0: 0},
         scratch_shapes=half_scratch + [pltpu.SemaphoreType.DMA((COMPS, 2))],
         compiler_params=PARAMS,
-    )(early, middle, early_got, cross, v_kept, cv_kept, restrict, prolong)
-    middle_got = swap(middle, lambda i: i % 2 == 1)
-    cross_local = cross
-    early, cross = pl.pallas_call(
-        late_kernel,
-        out_shape=(message, crosses),
-        in_specs=[ANY] + [VMEM] * 7,
-        out_specs=(VMEM, VMEM),
-        compiler_params=PARAMS,
-        cost_estimate=pl.CostEstimate(flops=10**9, bytes_accessed=10**7, transcendentals=0),
-    )(upper_fix, early, cross, v_kept, f_kept, c_kept, cv_kept, restrict)
-    late_got = swap(early, lambda i: i % 2 == 0 and i % deep == deep - 2)
-
+    )(left_sent, right_sent, inner_got, cross, *kept)
+    outer_got = lax.ppermute(left_sent, axes, outer)
     finish_scratch = half_scratch + [
         pltpu.SemaphoreType.DMA((COMPS, 2)),
         pltpu.VMEM((COMPS, 8 * HALF, LANES), F32),
         pltpu.SemaphoreType.DMA,
     ]
-    kept = (v_kept, cv_kept, restrict, prolong)
     corrected, fix = pl.pallas_call(
         lower_kernel,
         out_shape=(fine, coarse),
@@ -549,7 +486,7 @@
         input_output_aliases={0: 0},
         scratch_shapes=finish_scratch,
         compiler_params=PARAMS,
-    )(pinned(corrected), upper_fix, middle, middle_got, cross_local, *kept)
+    )(pinned(corrected), upper_fix, left_sent, right_got, cross, *kept)
     corrected, fix = pl.pallas_call(
         finish_kernel,
         out_shape=(fine, coarse),
@@ -558,7 +495,17 @@
         input_output_aliases={0: 0, 1: 1},
         scratch_shapes=finish_scratch,
         compiler_params=PARAMS,
-    )(pinned(corrected), pinned(fix), early, middle, middle_got, early_got, late_got, cross, *kept)
+    )(
+        pinned(corrected),
+        pinned(fix),
+        left_sent,
+        right_sent,
+        right_got,
+        inner_got,
+        outer_got,
+        cross,
+        *kept,
+    )
     corrected = corrected.reshape(COMPS, 2, TILES, 8, LANES)
     fix = fix.reshape(COMPS, BLOCKS, HALF, LANES)
     return (

time: 26.5 us -> 22.1 us (0.83)
  the two profiles are of different devices: /device:TPU:32 before, /device:TPU:56 now
where the time goes in v4:
time: 22.1 us; the launch traced here: 21.9 us
  starting transfers between devices  13 us (59%)
  Pallas kernels  6.46 us (29%)
  waiting for transfers between devices  1.75 us (8%)
  between operations  0.69 us (3%)
    ppermute x1, starting transfers between devices, shards(): outer_got = lax.ppermute(left_sent, axes, outer)  6.83 us
    ppermute x1, starting transfers between devices, shards(): lax.ppermute(right_sent, axes, [(i, i + 1) for i in range(count - 1)])  4.91 us
    pallas_call x1, Pallas kernels, shards(): pl.pallas_call(local_kernel, out_shape=(message, message, crosses, fine,...  2.74 us
    pallas_call x1, Pallas kernels, shards(): pl.pallas_call(lower_kernel, out_shape=(fine, coarse), in_specs=[HBM] + [...  1.82 us
    pallas_call x1, Pallas kernels, shards(): pl.pallas_call(upper_kernel, out_shape=(message, fine, jax.ShapeDtypeStru...  1.81 us
    ppermute x1, starting transfers between devices, shards(): inner_got = lax.ppermute(left_sent, axes, inner)  1.29 us
    ppermute x1, waiting for transfers between devices, shards(): inner_got = lax.ppermute(left_sent, axes, inner)  1.2 us
    ppermute x1, waiting for transfers between devices, shards(): lax.ppermute(right_sent, axes, [(i, i + 1) for i in range(count - 1)])  0.55 us
  transfers between devices with their start and end apart: 3, of which 2 were waited for; matrix products, arithmetic and copies ran while one was open for 0% of the time, Pallas kernels for 17%

profile of v4, /device:TPU:56, one launch (start us, length us, event | category | flops | bytes accessed | tf_op | source)
XLA Modules:
  0.0 21.9 jit_solution(12661791804009314124)
XLA Ops:
  0.6 2.7 %shard_map.59 = (f32[7,8,512]{2,1,0:T(8,128)S(1)}, f32[7,8,512]{2,1,0:T(8,128)S(1)}, f32[3,128,128]{2,1,0:T(8,128)S(1)}, f32[3,2,256,128]{3,2,1,0:T(8,128)S(1)},...) custom-call(f32[3,2,256,128]{3,2,1,0:T(8,128)} %bitcast.31, ...), custom_call_target="tpu_custom_call" | custom-call | tf_op jit(solution)/shard_map/pallas_call | solution.py:430
  3.4 1.3 %collective-permute-start = (f32[7,8,512]{2,1,0:T(8,128)S(1)}, f32[7,8,512]{2,1,0:T(8,128)S(1)}, u32[]{:S(2)}, u32[]{:S(2)}) collective-permute-start(f32[7,8,512]{2,1,0:T(8,128)S(1)} %get-tuple-element.16.left_in), channel_id=1, source_target_pairs={{1,0},{2,1},{3,2},{4,3},{5,4},{6,5},{9,8},{10,9},{11,10},{12,11},{... | collective-permute-start | bytes 344072 | tf_op jit(solution)/shard_map/ppermute | solution.py:461
  4.7 4.9 %collective-permute-start.1 = (f32[7,8,512]{2,1,0:T(8,128)S(1)}, f32[7,8,512]{2,1,0:T(8,128)S(1)}, u32[]{:S(2)}, u32[]{:S(2)}) collective-permute-start(f32[7,8,512]{2,1,0:T(8,128)S(1)} %get-tuple-element.17.right_sent), channel_id=1, source_target_pairs={{0,1},{1,2},{2,3},{3,4},{4,5},{5,6},{6,7},{7,8},{8,9},{9,10},{10,1... | collective-permute-start | bytes 344072 | tf_op jit(solution)/shard_map/ppermute | solution.py:460
  9.6 1.2 %collective-permute-done.inner_got = f32[7,8,512]{2,1,0:T(8,128)S(1)} collective-permute-done((f32[7,8,512]{2,1,0:T(8,128)S(1)}, f32[7,8,512]{2,1,0:T(8,128)S(1)}, u32[]{:S(2)}, u32[]{:S(2)}) %collective-permute-start) | collective-permute-done | bytes 114720 | tf_op jit(solution)/shard_map/ppermute | solution.py:461
  10.8 1.8 %shard_map.60 = (f32[7,8,512]{2,1,0:T(8,128)S(1)}, f32[3,2,256,128]{3,2,1,0:T(8,128)}, f32[3,32,128]{2,1,0:T(8,128)S(1)}) custom-call(f32[7,8,512]{2,1,0:T(8,128)S(1)} %get-tuple-element.16.left_in, f32[7,8,512]{2,1,0:T(8,128)S(1)} %get-tuple-element.17.right_sent, f32[7,8,512]{2,1,0:T(8,128)S(1)} %collective-permute-done.inner_got, ...), custom_call_target="tpu_custom_call", output_to_operand_aliasing={{0}: (0, {})} | custom-call | tf_op jit(solution)/shard_map/pallas_call | solution.py:466
  12.6 6.8 %collective-permute-start.2 = (f32[7,8,512]{2,1,0:T(8,128)S(1)}, f32[7,8,512]{2,1,0:T(8,128)S(1)}, u32[]{:S(2)}, u32[]{:S(2)}) collective-permute-start(f32[7,8,512]{2,1,0:T(8,128)S(1)} %get-tuple-element.25.left_sent), channel_id=1, source_target_pairs={{7,6},{8,7},{15,14},{16,15},{23,22},{24,23},{31,30},{32,31},{39,38... | collective-permute-start | bytes 344072 | tf_op jit(solution)/shard_map/ppermute | solution.py:475
  19.5 0.5 %collective-permute-done.1.right_got = f32[7,8,512]{2,1,0:T(8,128)S(1)} collective-permute-done((f32[7,8,512]{2,1,0:T(8,128)S(1)}, f32[7,8,512]{2,1,0:T(8,128)S(1)}, u32[]{:S(2)}, u32[]{:S(2)}) %collective-permute-start.1) | collective-permute-done | bytes 114720 | tf_op jit(solution)/shard_map/ppermute | solution.py:460
  20.0 1.8 %shard_map.61 = (f32[3,2,256,128]{3,2,1,0:T(8,128)}, f32[3,64,128]{2,1,0:T(8,128)}) custom-call(f32[3,2,256,128]{3,2,1,0:T(8,128)} %get-tuple-element.23.out_in, f32[3,32,128]{2,1,0:T(8,128)S(1)} %get-tuple-element.24.upper_fix, f32[7,8,512]{2,1,0:T(8,128)S(1)} %get-tuple-element.25.left_sent, ...), custom_call_target="tpu_custom_call", output_to_operand_aliasing={{0}: (0, {})} | custom-call | tf_op jit(solution)/shard_map/pallas_call | solution.py:481
  21.8 0.0 collective-permute-done.2.outer_got
  21.8 0.1 shard_map.62
Async XLA Ops:
  3.4 7.4 %collective-permute-start = (f32[7,8,512]{2,1,0:T(8,128)S(1)}, f32[7,8,512]{2,1,0:T(8,128)S(1)}, u32[]{:S(2)}, u32[]{:S(2)}) collective-permute-start(f32[7,8,512]{2,1,0:T(8,128)S(1)} %get-tuple-element.16.left_in), channel_id=1, source_target_pairs={{1,0},{2,1},{3,2},{4,3},{5,4},{6,5},{9,8},{10,9},{11,10},{12,11},{... | collective-permute-start | bytes 344072 | tf_op jit(solution)/shard_map/ppermute | solution.py:461
  4.7 15.3 %collective-permute-start.1 = (f32[7,8,512]{2,1,0:T(8,128)S(1)}, f32[7,8,512]{2,1,0:T(8,128)S(1)}, u32[]{:S(2)}, u32[]{:S(2)}) collective-permute-start(f32[7,8,512]{2,1,0:T(8,128)S(1)} %get-tuple-element.17.right_sent), channel_id=1, source_target_pairs={{0,1},{1,2},{2,3},{3,4},{4,5},{5,6},{6,7},{7,8},{8,9},{9,10},{10,1... | collective-permute-start | bytes 344072 | tf_op jit(solution)/shard_map/ppermute | solution.py:460
  12.6 9.2 %collective-permute-start.2 = (f32[7,8,512]{2,1,0:T(8,128)S(1)}, f32[7,8,512]{2,1,0:T(8,128)S(1)}, u32[]{:S(2)}, u32[]{:S(2)}) collective-permute-start(f32[7,8,512]{2,1,0:T(8,128)S(1)} %get-tuple-element.25.left_sent), channel_id=1, source_target_pairs={{7,6},{8,7},{15,14},{16,15},{23,22},{24,23},{31,30},{32,31},{39,38... | collective-permute-start | bytes 344072 | tf_op jit(solution)/shard_map/ppermute | solution.py:475

commit v5 on v2

--- a/solution.py
+++ b/solution.py
@@ -80,8 +80,8 @@
     f_hbm,
     c_hbm,
     cv_hbm,
-    right_ref,
-    left_ref,
+    near_ref,
+    far_ref,
     src_ref,
     v_ref,
     cv_ref,
@@ -100,6 +100,7 @@
     for copy in copies:
         copy.start()
 
+    even = lax.rem(lax.axis_index("sub"), 2) == 0
     row, lane = iotas(PLANES)
     low_half = lane < 64
     first_col = lane % 64 == 0
@@ -108,10 +109,14 @@
     fill_prolong(q_ref)
     matrix = w_ref[...]
 
+    def send(slab, lanes, to_left, to_right):
+        near_ref[slab, :, lanes] = jnp.where(even, to_right, to_left)
+        far_ref[slab, :, lanes] = jnp.where(even, to_left, to_right)
+
     def packed_planes(slab, source):
         for part in range(4):
-            left_ref[slab, :, tile(part)] = source[0, pl.ds(8 * part, 8, 32), :]
-            right_ref[slab, :, tile(part)] = source[1, pl.ds(8 * part + 7, 8, 32), :]
+            first = source[0, pl.ds(8 * part, 8, 32), :]
+            send(slab, tile(part), first, source[1, pl.ds(8 * part + 7, 8, 32), :])
 
     copies[0].wait()
     packed_planes(COMPS, c_vm)
@@ -154,32 +159,65 @@
             src_ref[k, eight(j), :] = source
             sources.append(source)
         for j in range(3):
-            left_ref[4 + j, :, tile(k)] = sources[j]
-            right_ref[4 + j, :, tile(k)] = (sources[6:] + half_odds[-1:])[j]
+            send(4 + j, tile(k), sources[j], (sources[6:] + half_odds[-1:])[j])
         packed_planes(k, v_ref.at[k])
 
     copies[-1].wait()
     for j in range(3):
-        left_ref[4 + j, :, tile(COMPS)] = cv_ref[pl.ds(j, 8, 8), :]
-        right_ref[4 + j, :, tile(COMPS)] = cv_ref[pl.ds(min(6 + j, 7), 8, 8), :]
+        first = cv_ref[pl.ds(j, 8, 8), :]
+        send(4 + j, tile(COMPS), first, cv_ref[pl.ds(min(6 + j, 7), 8, 8), :])
 
 
 def finish_kernel(
     v_ref,
     cv_ref,
     src_ref,
-    right_sent,
-    left_sent,
-    right_got,
-    left_got,
+    near_sent,
+    far_sent,
+    near_hbm,
+    far_hbm,
     w_ref,
     q_ref,
     out_hbm,
-    fix_ref,
+    fix_hbm,
+    near_got,
+    far_got,
+    got_sems,
     out_vm,
     mix_vm,
     sems,
+    fix_ref,
+    fix_sem,
 ):
+    at_sub, at_grp = lax.axis_index("sub"), lax.axis_index("grp")
+    odd = lax.rem(at_sub, 2)
+    even = odd == 0
+    fetches = [
+        pltpu.make_async_copy(far_hbm.at[odd], far_got, got_sems.at[0]),
+        pltpu.make_async_copy(near_hbm.at[1 - odd], near_got, got_sems.at[1]),
+    ]
+    for fetch in fetches:
+        fetch.start()
+    for fetch in fetches:
+        fetch.wait()
+    begin = (at_sub == 0) & (at_grp == 0)
+    end = (at_sub == lax.axis_size("sub") - 1) & (at_grp == lax.axis_size("grp") - 1)
+
+    def left_sent(slab, lanes):
+        return jnp.where(even, far_sent[slab, :, lanes], near_sent[slab, :, lanes])
+
+    def right_sent(slab, lanes):
+        return jnp.where(even, near_sent[slab, :, lanes], far_sent[slab, :, lanes])
+
+    def right_got(slab, lanes):
+        value = jnp.where(even, far_got[slab, :, lanes], near_got[slab, :, lanes])
+        return jnp.where(begin, 0.0, value)
+
+    def left_got(slab, lanes):
+        value = jnp.where(even, near_got[slab, :, lanes], far_got[slab, :, lanes])
+        return jnp.where(end, 0.0, value)
+
+    whole = slice(0, WIDE)
     _, lane = iotas(8)
     kept_up = lane < LANES - NZ
     kept_down = lane >= NZ
@@ -188,8 +226,9 @@
 
     rows = []
     for sent, got in ((left_sent, right_got), (right_sent, left_got)):
-        rows += [got[k] * sent[COMPS] for k in range(COMPS)]
-        rows += [sent[k] * got[COMPS] for k in range(COMPS)]
+        own_coeff, their_coeff = sent(COMPS, whole), got(COMPS, whole)
+        rows += [got(k, whole) * own_coeff for k in range(COMPS)]
+        rows += [sent(k, whole) * their_coeff for k in range(COMPS)]
     sums = split_dot(jnp.concatenate(rows, axis=0), w_ref[...])
     terms = []
     for part in range(len(rows)):
@@ -200,11 +239,11 @@
     inverse, quotient = {}, {}
     for j in range(first, last + 1):
         if j < 0:
-            coeff = right_got[6 + j, :, tile(COMPS)]
+            coeff = right_got(6 + j, tile(COMPS))
         elif j < HALF:
             coeff = cv_ref[pl.ds(j, 8, 8), :]
         else:
-            coeff = left_got[4 + j - HALF, :, tile(COMPS)]
+            coeff = left_got(4 + j - HALF, tile(COMPS))
         if j == HALF:
             inside = coeff > 0.0
         inverse[j] = 1.0 / (1.0 + 6.0 * coeff)
@@ -228,14 +267,14 @@
         left_theirs, left_ours = terms[k], terms[COMPS + k]
         right_theirs, right_ours = terms[2 * COMPS + k], terms[3 * COMPS + k]
         source = {j: src_ref[k, eight(j), :] for j in range(HALF)}
-        source[-2] = right_got[4, :, at]
-        source[-1] = right_got[5, :, at] + 0.0625 * left_ours
-        source[0] += right_got[6, :, at] + (0.125 * left_theirs + 0.0625 * left_ours)
+        source[-2] = right_got(4, at)
+        source[-1] = right_got(5, at) + 0.0625 * left_ours
+        source[0] += right_got(6, at) + (0.125 * left_theirs + 0.0625 * left_ours)
         source[HALF - 1] += 0.0625 * right_theirs
-        after = right_sent[6, :, at] + left_got[4, :, at] + (0.0625 * right_theirs + 0.125 * right_ours)
+        after = right_sent(6, at) + left_got(4, at) + (0.0625 * right_theirs + 0.125 * right_ours)
         source[HALF] = jnp.where(inside, after, 0.0)
-        source[HALF + 1] = left_got[5, :, at]
-        source[HALF + 2] = left_got[6, :, at]
+        source[HALF + 1] = left_got(5, at)
+        source[HALF + 2] = left_got(6, at)
 
         scaled = {j: source[j] * inverse[j] for j in source}
         update = {j: x * (1.0 / CENTER) for j, x in scaled.items()}
@@ -273,6 +312,8 @@
         store = pltpu.make_async_copy(out_vm.at[k], out_hbm.at[k], sems.at[k])
         store.start()
         stores.append(store)
+    stores.append(pltpu.make_async_copy(fix_ref, fix_hbm, fix_sem))
+    stores[-1].start()
     for store in stores:
         store.wait()
 
@@ -291,6 +332,10 @@
 
 def pinned(field):
     return pltpu.with_memory_space_constraint(fine_tiled(field), pltpu.HBM)
+
+
+def pinned_as_is(field):
+    return pltpu.with_memory_space_constraint(field, pltpu.HBM)
 
 
 def shards(velocity, forcing, viscosity, coarse_visc):
@@ -299,7 +344,7 @@
     message = jax.ShapeDtypeStruct((7, 8, WIDE), F32)
     fine = jax.ShapeDtypeStruct((COMPS,) + FINE_TILED, F32)
     coarse = jax.ShapeDtypeStruct((COMPS, 8 * HALF, LANES), F32)
-    right_sent, left_sent, source, kept, coeffs, restrict, prolong = pl.pallas_call(
+    near_sent, far_sent, source, kept, coeffs, restrict, prolong = pl.pallas_call(
         local_kernel,
         out_shape=(
             message,
@@ -323,22 +368,28 @@
 
     axes = ("grp", "sub")
     count = lax.axis_size(axes)
-    forward = [(i, i + 1) for i in range(count - 1)]
-    right_got = lax.ppermute(right_sent, axes, forward)
-    left_got = lax.ppermute(left_sent, axes, [(j, i) for i, j in forward])
+    near = [[i, i + 1] for i in range(0, count, 2)]
+    far = [[i, (i + 1) % count] for i in range(1, count, 2)]
+    far_got = lax.all_gather(far_sent, axes, axis_index_groups=far)
+    near_got = lax.all_gather(near_sent, axes, axis_index_groups=near)
 
     corrected, fix = pl.pallas_call(
         finish_kernel,
         out_shape=(fine, coarse),
-        in_specs=[VMEM] * 9,
-        out_specs=(HBM, VMEM),
+        in_specs=[VMEM] * 5 + [HBM] * 2 + [VMEM] * 2,
+        out_specs=(HBM, HBM),
         scratch_shapes=[
+            pltpu.VMEM(message.shape, F32),
+            pltpu.VMEM(message.shape, F32),
+            pltpu.SemaphoreType.DMA((2,)),
             pltpu.VMEM((COMPS,) + FINE_TILED, F32),
             pltpu.VMEM((COMPS, 8 * PLANES, LANES), F32),
             pltpu.SemaphoreType.DMA((COMPS,)),
+            pltpu.VMEM((COMPS, 8 * HALF, LANES), F32),
+            pltpu.SemaphoreType.DMA,
         ],
         compiler_params=pltpu.CompilerParams(vmem_limit_bytes=LIMIT),
-    )(kept, coeffs, source, right_sent, left_sent, right_got, left_got, restrict, prolong)
+    )(kept, coeffs, source, near_sent, far_sent, pinned_as_is(near_got), pinned_as_is(far_got), restrict, prolong)
     corrected = corrected.reshape(COMPS, 2, TILES, 8, LANES)
     fix = fix.reshape(COMPS, BLOCKS, HALF, LANES)
     return (

time: 23.8 us -> 26 us (1.092)
  blocking collectives: 0 us -> 19.5 us
  starting transfers between devices: 15.3 us -> 0 us
  waiting for transfers between devices: 2.35 us -> 0 us
  Pallas kernels: 5.33 us -> 5.67 us
    all_gather x0 -> x2, blocking collectives: none -> 19.5 us  [the longest x1 13.2 us: shards(): far_got = lax.all_gather(far_sent, axes, axis_index_groups=far)]
    ppermute x2 -> x0, starting transfers between devices: 15.3 us -> none  [the longest x1 11 us: shards(): left_got = lax.ppermute(left_sent, axes, [(j, i) for i, j in forward])]
    ppermute x2 -> x0, waiting for transfers between devices: 2.35 us -> none  [the longest x1 1.71 us: shards(): left_got = lax.ppermute(left_sent, axes, [(j, i) for i, j in forward])]
    pallas_call x1, Pallas kernels: 2.57 us -> 2.91 us  [shards(): pl.pallas_call(finish_kernel, out_shape=(fine, coarse), in_specs=[VMEM] *...]
  transfers between devices with their start and end apart: 2 -> 0, of which waited for: 2 -> 0; matrix products, arithmetic and copies ran while one was open for 0% -> 0% of each run, Pallas kernels for 0% -> 0%
where the time goes in v5:
time: 26 us; the launch traced here: 25.8 us
  blocking collectives  19.5 us (75%)
  Pallas kernels  5.67 us (22%)
  between operations  0.64 us (2%)
    all_gather x1, blocking collectives, shards(): far_got = lax.all_gather(far_sent, axes, axis_index_groups=far)  13.2 us
    all_gather x1, blocking collectives, shards(): near_got = lax.all_gather(near_sent, axes, axis_index_groups=near)  6.27 us
    pallas_call x1, Pallas kernels, shards(): pl.pallas_call(finish_kernel, out_shape=(fine, coarse), in_specs=[VMEM] *...  2.91 us
    pallas_call x1, Pallas kernels, shards(): pl.pallas_call(local_kernel, out_shape=(message, message, coarse, fine, j...  2.76 us

profile of v5, /device:TPU:56, one launch (start us, length us, event | category | flops | bytes accessed | tf_op | source)
XLA Modules:
  0.0 25.8 jit_solution(4183508799422757837)
XLA Ops:
  0.6 2.8 %shard_map.59 = (f32[7,8,512]{2,1,0:T(8,128)S(1)}, f32[7,8,512]{2,1,0:T(8,128)S(1)}, f32[3,64,128]{2,1,0:T(8,128)S(1)}, f32[3,2,256,128]{3,2,1,0:T(8,128)S(1)}, ...) custom-call(f32[3,2,256,128]{3,2,1,0:T(8,128)} %bitcast.34, ...), custom_call_target="tpu_custom_call" | custom-call | tf_op jit(solution)/shard_map/pallas_call | solution.py:347
  3.4 6.3 %all-gather = f32[14,8,512]{2,1,0:T(8,128)} all-gather(f32[7,8,512]{2,1,0:T(8,128)S(1)} %get-tuple-element.14.near_sent), channel_id=2, replica_groups={{0,1},{2,3},{4,5},{6,7},{8,9},{10,11},{12,13},{14,15},{16,17},{18,19},{..., dimensions={0}, use_global_device_ids=true | all-gather | bytes 344064 | tf_op jit(solution)/shard_map/all_gather | solution.py:374
  9.7 13.2 %all-gather.1 = f32[14,8,512]{2,1,0:T(8,128)} all-gather(f32[7,8,512]{2,1,0:T(8,128)S(1)} %get-tuple-element.15.far_sent), channel_id=3, replica_groups={{1,2},{3,4},{5,6},{7,8},{9,10},{11,12},{13,14},{15,16},{17,18},{19,20},..., dimensions={0}, use_global_device_ids=true | all-gather | bytes 344064 | tf_op jit(solution)/shard_map/all_gather | solution.py:373
  22.9 2.9 %shard_map.60 = (f32[3,2,256,128]{3,2,1,0:T(8,128)}, f32[3,64,128]{2,1,0:T(8,128)}) custom-call(f32[3,2,256,128]{3,2,1,0:T(8,128)S(1)} %get-tuple-element.11.v_ref, f32[64,128]{1,0:T(8,128)S(1)} %get-tuple-element.12.cv_ref, f32[3,64,128]{2,1,0:T(8,128)S(1)} %get-tuple-element.13.src_ref, f32[7,8,512]{2,1,0:T(8,128)S(1)} %get-tuple-element.14.near_sent, ...), custom_call_target="tpu_custom_call" | custom-call | tf_op jit(solution)/shard_map/pallas_call | solution.py:376

commit v6 on v4

--- a/solution.py
+++ b/solution.py
@@ -57,12 +57,15 @@
             ref[NZ * row : NZ * (row + 1), tile(part)] = kept.astype(BF16)
 
 
+def halves(values):
+    high = values.astype(BF16)
+    return high, (values - high.astype(F32)).astype(BF16)
+
+
 def split_dot(left, matrix):
-    high = left.astype(BF16)
-    low = (left - high.astype(F32)).astype(BF16)
-    return jnp.dot(high, matrix, preferred_element_type=F32) + jnp.dot(
-        low, matrix, preferred_element_type=F32
-    )
+    rows = left.shape[0]
+    sums = jnp.dot(jnp.concatenate(halves(left), axis=0), matrix, preferred_element_type=F32)
+    return sums[:rows] + sums[rows:]
 
 
 def iotas(rows):
@@ -89,6 +92,7 @@
     q_ref,
     f_vm,
     c_vm,
+    split_vm,
     sems,
 ):
     copies = [pltpu.make_async_copy(c_hbm, c_vm, sems.at[0])]
@@ -105,7 +109,6 @@
     last_col = lane % 64 == 63
     fill_restrict(w_ref)
     fill_prolong(q_ref)
-    matrix = w_ref[...]
 
     def packed_planes(slab, source):
         for part in range(4):
@@ -124,9 +127,8 @@
 
         values = [planes_of(v_ref.at[k], t) for t in range(TILES)]
         swapped = [pltpu.roll(x, 64, 1) for x in values]
-        blocks = []
         for s in range(BLOCKS):
-            pieces = []
+            at = slice(PLANES * (BLOCKS * k + s), PLANES * (BLOCKS * k + s + 1))
             for t in range(4 * s, 4 * s + 4):
                 x, turned = values[t], swapped[t]
                 beside = turned + jnp.where(low_half, swapped[t - 1], swapped[(t + 1) % TILES])
@@ -134,15 +136,20 @@
                 beside += pltpu.roll(jnp.where(first_col, turned, x), LANES - 1, 1)
                 beside += jnp.where(row == 0, 0.0, pltpu.roll(x, 1, 0))
                 beside += jnp.where(row == PLANES - 1, 0.0, pltpu.roll(x, PLANES - 1, 0))
-                pieces.append(
-                    planes_of(f_vm.at[k], t) - x + planes_of(c_vm, t) * (beside - 6.0 * x)
-                )
-            blocks.append(jnp.concatenate(pieces, axis=1))
-        sums = split_dot(jnp.concatenate(blocks, axis=0), matrix)
-        parts = [sums[PLANES * s : PLANES * (s + 1)] for s in range(BLOCKS)]
+                residual = planes_of(f_vm.at[k], t) - x + planes_of(c_vm, t) * (beside - 6.0 * x)
+                for part, value in enumerate(halves(residual)):
+                    split_vm[part, at, tile(t % 4)] = value
+
+    matrix = w_ref[...]
+    sums = jnp.dot(split_vm[0], matrix, preferred_element_type=F32)
+    sums += jnp.dot(split_vm[1], matrix, preferred_element_type=F32)
+    for k in range(COMPS):
+        mine = sums[PLANES * BLOCKS * k : PLANES * BLOCKS * (k + 1)]
+        parts = [mine[PLANES * s : PLANES * (s + 1)] for s in range(BLOCKS)]
         for s in range(BLOCKS):
             crossed = parts[s][:, :LANES] + parts[s - 1][:, LANES:]
             cross_ref[k, PLANES * s : PLANES * (s + 1), :] = crossed
+    for k in range(COMPS):
         planes = [cross_ref[k, pl.ds(p, 8, PLANES), :] for p in range(PLANES)]
         half_odds = [0.0625 * planes[2 * j + 1] for j in range(HALF)]
         sources = []
@@ -206,7 +213,6 @@
         return total
 
     sigma = CENTER / HALF_WIDTH
-    stores = []
     for k in range(COMPS):
         at = tile(k)
         theirs, ours = terms[k], terms[COMPS + k]
@@ -252,13 +258,17 @@
             keep_fix(k, i, here)
             mix_vm[k, eight(2 * i), :] = here
             mix_vm[k, eight(2 * i + 1), :] = 0.5 * (here + after)
+    left = []
+    for k in range(COMPS):
         mixed = [mix_vm[k, pl.ds(s, 8, 8), :] for s in range(BLOCKS)]
-        left = [
+        left += [
             jnp.concatenate([mixed[s], mixed[(s + 1) % BLOCKS]], axis=1) for s in range(BLOCKS)
         ]
-        fine = split_dot(jnp.concatenate(left, axis=0), q_ref[...])
+    fine = split_dot(jnp.concatenate(left, axis=0), q_ref[...])
+    stores = []
+    for k in range(COMPS):
         for t in range(TILES):
-            add = fine[eight(t // 4), tile(t % 4)]
+            add = fine[eight(BLOCKS * k + t // 4), tile(t % 4)]
             out_vm[k, h, eight(t), :] = v_ref[k, h, eight(t), :] + add
         store = pltpu.make_async_copy(out_vm.at[k, h], out_hbm.at[k, h], sems.at[k, h])
         store.start()
@@ -443,6 +453,7 @@
         scratch_shapes=[
             pltpu.VMEM((COMPS,) + FINE_TILED, F32),
             pltpu.VMEM(FINE_TILED, F32),
+            pltpu.VMEM((2, COMPS * BLOCKS * PLANES, WIDE), BF16),
             pltpu.SemaphoreType.DMA((2 + 2 * COMPS,)),
         ],
         compiler_params=PARAMS,

time: 22.1 us -> 21.7 us (0.982)
  Pallas kernels: 6.46 us -> 5.58 us
  starting transfers between devices: 13 us -> 13.3 us
  waiting for transfers between devices: 1.75 us -> 1.98 us
    pallas_call x1, Pallas kernels: 2.74 us -> 2.44 us  [shards(): pl.pallas_call(local_kernel, out_shape=(message, message, crosses, fine,...]
    ppermute x1, starting transfers between devices: 6.83 us -> 7.11 us  [shards(): outer_got = lax.ppermute(left_sent, axes, outer)]
    pallas_call x1, Pallas kernels: 1.81 us -> 1.53 us  [shards(): pl.pallas_call(upper_kernel, out_shape=(message, fine, jax.ShapeDtypeStru...]
    pallas_call x1, Pallas kernels: 1.82 us -> 1.55 us  [shards(): pl.pallas_call(lower_kernel, out_shape=(fine, coarse), in_specs=[HBM] + [...]
    ppermute x1, waiting for transfers between devices: 0.01 us -> 0.24 us  [shards(): outer_got = lax.ppermute(left_sent, axes, outer)]
  transfers between devices with their start and end apart: 3 -> 3, of which waited for: 2 -> 3; matrix products, arithmetic and copies ran while one was open for 0% -> 0% of each run, Pallas kernels for 17% -> 14%
where the time goes in v6:
time: 21.7 us; the launch traced here: 21.6 us
  starting transfers between devices  13.3 us (61%)
  Pallas kernels  5.58 us (26%)
  waiting for transfers between devices  1.98 us (9%)
  between operations  0.68 us (3%)
    ppermute x1, starting transfers between devices, shards(): outer_got = lax.ppermute(left_sent, axes, outer)  7.11 us
    ppermute x1, starting transfers between devices, shards(): lax.ppermute(right_sent, axes, [(i, i + 1) for i in range(count - 1)])  4.91 us
    pallas_call x1, Pallas kernels, shards(): pl.pallas_call(local_kernel, out_shape=(message, message, crosses, fine,...  2.44 us
    pallas_call x1, Pallas kernels, shards(): pl.pallas_call(lower_kernel, out_shape=(fine, coarse), in_specs=[HBM] + [...  1.55 us
    pallas_call x1, Pallas kernels, shards(): pl.pallas_call(upper_kernel, out_shape=(message, fine, jax.ShapeDtypeStru...  1.53 us
    ppermute x1, starting transfers between devices, shards(): inner_got = lax.ppermute(left_sent, axes, inner)  1.29 us
    ppermute x1, waiting for transfers between devices, shards(): inner_got = lax.ppermute(left_sent, axes, inner)  1.2 us
    ppermute x1, waiting for transfers between devices, shards(): lax.ppermute(right_sent, axes, [(i, i + 1) for i in range(count - 1)])  0.55 us
  transfers between devices with their start and end apart: 3, of which 3 were waited for; matrix products, arithmetic and copies ran while one was open for 0% of the time, Pallas kernels for 14%

profile of v6, /device:TPU:56, one launch (start us, length us, event | category | flops | bytes accessed | tf_op | source)
XLA Modules:
  0.0 21.6 jit_solution(9115167890885413549)
XLA Ops:
  0.6 2.4 %shard_map.59 = (f32[7,8,512]{2,1,0:T(8,128)S(1)}, f32[7,8,512]{2,1,0:T(8,128)S(1)}, f32[3,128,128]{2,1,0:T(8,128)S(1)}, f32[3,2,256,128]{3,2,1,0:T(8,128)S(1)},...) custom-call(f32[3,2,256,128]{3,2,1,0:T(8,128)} %bitcast.31, ...), custom_call_target="tpu_custom_call" | custom-call | tf_op jit(solution)/shard_map/pallas_call | solution.py:440
  3.1 1.3 %collective-permute-start = (f32[7,8,512]{2,1,0:T(8,128)S(1)}, f32[7,8,512]{2,1,0:T(8,128)S(1)}, u32[]{:S(2)}, u32[]{:S(2)}) collective-permute-start(f32[7,8,512]{2,1,0:T(8,128)S(1)} %get-tuple-element.16.left_in), channel_id=1, source_target_pairs={{1,0},{2,1},{3,2},{4,3},{5,4},{6,5},{9,8},{10,9},{11,10},{12,11},{... | collective-permute-start | bytes 344072 | tf_op jit(solution)/shard_map/ppermute | solution.py:472
  4.4 4.9 %collective-permute-start.1 = (f32[7,8,512]{2,1,0:T(8,128)S(1)}, f32[7,8,512]{2,1,0:T(8,128)S(1)}, u32[]{:S(2)}, u32[]{:S(2)}) collective-permute-start(f32[7,8,512]{2,1,0:T(8,128)S(1)} %get-tuple-element.17.right_sent), channel_id=1, source_target_pairs={{0,1},{1,2},{2,3},{3,4},{4,5},{5,6},{6,7},{7,8},{8,9},{9,10},{10,1... | collective-permute-start | bytes 344072 | tf_op jit(solution)/shard_map/ppermute | solution.py:471
  9.3 1.2 %collective-permute-done.inner_got = f32[7,8,512]{2,1,0:T(8,128)S(1)} collective-permute-done((f32[7,8,512]{2,1,0:T(8,128)S(1)}, f32[7,8,512]{2,1,0:T(8,128)S(1)}, u32[]{:S(2)}, u32[]{:S(2)}) %collective-permute-start) | collective-permute-done | bytes 114720 | tf_op jit(solution)/shard_map/ppermute | solution.py:472
  10.5 1.5 %shard_map.60 = (f32[7,8,512]{2,1,0:T(8,128)S(1)}, f32[3,2,256,128]{3,2,1,0:T(8,128)}, f32[3,32,128]{2,1,0:T(8,128)S(1)}) custom-call(f32[7,8,512]{2,1,0:T(8,128)S(1)} %get-tuple-element.16.left_in, f32[7,8,512]{2,1,0:T(8,128)S(1)} %get-tuple-element.17.right_sent, f32[7,8,512]{2,1,0:T(8,128)S(1)} %collective-permute-done.inner_got, ...), custom_call_target="tpu_custom_call", output_to_operand_aliasing={{0}: (0, {})} | custom-call | tf_op jit(solution)/shard_map/pallas_call | solution.py:477
  12.0 7.1 %collective-permute-start.2 = (f32[7,8,512]{2,1,0:T(8,128)S(1)}, f32[7,8,512]{2,1,0:T(8,128)S(1)}, u32[]{:S(2)}, u32[]{:S(2)}) collective-permute-start(f32[7,8,512]{2,1,0:T(8,128)S(1)} %get-tuple-element.25.left_sent), channel_id=1, source_target_pairs={{7,6},{8,7},{15,14},{16,15},{23,22},{24,23},{31,30},{32,31},{39,38... | collective-permute-start | bytes 344072 | tf_op jit(solution)/shard_map/ppermute | solution.py:486
  19.2 0.5 %collective-permute-done.1.right_got = f32[7,8,512]{2,1,0:T(8,128)S(1)} collective-permute-done((f32[7,8,512]{2,1,0:T(8,128)S(1)}, f32[7,8,512]{2,1,0:T(8,128)S(1)}, u32[]{:S(2)}, u32[]{:S(2)}) %collective-permute-start.1) | collective-permute-done | bytes 114720 | tf_op jit(solution)/shard_map/ppermute | solution.py:471
  19.7 1.5 %shard_map.61 = (f32[3,2,256,128]{3,2,1,0:T(8,128)}, f32[3,64,128]{2,1,0:T(8,128)}) custom-call(f32[3,2,256,128]{3,2,1,0:T(8,128)} %get-tuple-element.23.out_in, f32[3,32,128]{2,1,0:T(8,128)S(1)} %get-tuple-element.24.upper_fix, f32[7,8,512]{2,1,0:T(8,128)S(1)} %get-tuple-element.25.left_sent, ...), custom_call_target="tpu_custom_call", output_to_operand_aliasing={{0}: (0, {})} | custom-call | tf_op jit(solution)/shard_map/pallas_call | solution.py:492
  21.3 0.2 %collective-permute-done.2.outer_got = f32[7,8,512]{2,1,0:T(8,128)S(1)} collective-permute-done((f32[7,8,512]{2,1,0:T(8,128)S(1)}, f32[7,8,512]{2,1,0:T(8,128)S(1)}, u32[]{:S(2)}, u32[]{:S(2)}) %collective-permute-start.2) | collective-permute-done | bytes 114720 | tf_op jit(solution)/shard_map/ppermute | solution.py:486
  21.5 0.1 shard_map.62
Async XLA Ops:
  3.1 7.4 %collective-permute-start = (f32[7,8,512]{2,1,0:T(8,128)S(1)}, f32[7,8,512]{2,1,0:T(8,128)S(1)}, u32[]{:S(2)}, u32[]{:S(2)}) collective-permute-start(f32[7,8,512]{2,1,0:T(8,128)S(1)} %get-tuple-element.16.left_in), channel_id=1, source_target_pairs={{1,0},{2,1},{3,2},{4,3},{5,4},{6,5},{9,8},{10,9},{11,10},{12,11},{... | collective-permute-start | bytes 344072 | tf_op jit(solution)/shard_map/ppermute | solution.py:472
  4.4 15.3 %collective-permute-start.1 = (f32[7,8,512]{2,1,0:T(8,128)S(1)}, f32[7,8,512]{2,1,0:T(8,128)S(1)}, u32[]{:S(2)}, u32[]{:S(2)}) collective-permute-start(f32[7,8,512]{2,1,0:T(8,128)S(1)} %get-tuple-element.17.right_sent), channel_id=1, source_target_pairs={{0,1},{1,2},{2,3},{3,4},{4,5},{5,6},{6,7},{7,8},{8,9},{9,10},{10,1... | collective-permute-start | bytes 344072 | tf_op jit(solution)/shard_map/ppermute | solution.py:471
  12.0 9.5 %collective-permute-start.2 = (f32[7,8,512]{2,1,0:T(8,128)S(1)}, f32[7,8,512]{2,1,0:T(8,128)S(1)}, u32[]{:S(2)}, u32[]{:S(2)}) collective-permute-start(f32[7,8,512]{2,1,0:T(8,128)S(1)} %get-tuple-element.25.left_sent), channel_id=1, source_target_pairs={{7,6},{8,7},{15,14},{16,15},{23,22},{24,23},{31,30},{32,31},{39,38... | collective-permute-start | bytes 344072 | tf_op jit(solution)/shard_map/ppermute | solution.py:486

commit v7 on v6

--- a/solution.py
+++ b/solution.py
@@ -93,15 +93,22 @@
     f_vm,
     c_vm,
     split_vm,
+    beside_vm,
     sems,
 ):
-    copies = [pltpu.make_async_copy(c_hbm, c_vm, sems.at[0])]
-    for k in range(COMPS):
-        copies.append(pltpu.make_async_copy(v_hbm.at[k], v_ref.at[k], sems.at[1 + 2 * k]))
-        copies.append(pltpu.make_async_copy(f_hbm.at[k], f_vm.at[k], sems.at[2 + 2 * k]))
-    copies.append(pltpu.make_async_copy(cv_hbm, cv_ref, sems.at[1 + 2 * COMPS]))
-    for copy in copies:
-        copy.start()
+    c_copy = pltpu.make_async_copy(c_hbm, c_vm, sems.at[0])
+    cv_copy = pltpu.make_async_copy(cv_hbm, cv_ref, sems.at[1])
+    v_copies, f_copies = [], []
+    for k in range(COMPS):
+        v_copies.append(pltpu.make_async_copy(v_hbm.at[k], v_ref.at[k], sems.at[2 + 2 * k]))
+        f_copies.append(pltpu.make_async_copy(f_hbm.at[k], f_vm.at[k], sems.at[3 + 2 * k]))
+    v_copies[0].start()
+    c_copy.start()
+    for k in range(COMPS):
+        if k > 0:
+            v_copies[k].start()
+        f_copies[k].start()
+    cv_copy.start()
 
     row, lane = iotas(PLANES)
     low_half = lane < 64
@@ -115,30 +122,32 @@
             left_ref[slab, :, tile(part)] = source[0, pl.ds(8 * part, 8, 32), :]
             right_ref[slab, :, tile(part)] = source[1, pl.ds(8 * part + 7, 8, 32), :]
 
-    copies[0].wait()
-    packed_planes(COMPS, c_vm)
-
-    for k in range(COMPS):
-        copies[1 + 2 * k].wait()
-        copies[2 + 2 * k].wait()
+    for k in range(COMPS):
+        v_copies[k].wait()
 
         def planes_of(ref, t):
             return jnp.concatenate([ref[0, eight(t), :], ref[1, eight(t), :]], axis=0)
 
         values = [planes_of(v_ref.at[k], t) for t in range(TILES)]
         swapped = [pltpu.roll(x, 64, 1) for x in values]
-        for s in range(BLOCKS):
-            at = slice(PLANES * (BLOCKS * k + s), PLANES * (BLOCKS * k + s + 1))
-            for t in range(4 * s, 4 * s + 4):
-                x, turned = values[t], swapped[t]
-                beside = turned + jnp.where(low_half, swapped[t - 1], swapped[(t + 1) % TILES])
-                beside += pltpu.roll(jnp.where(last_col, turned, x), 1, 1)
-                beside += pltpu.roll(jnp.where(first_col, turned, x), LANES - 1, 1)
-                beside += jnp.where(row == 0, 0.0, pltpu.roll(x, 1, 0))
-                beside += jnp.where(row == PLANES - 1, 0.0, pltpu.roll(x, PLANES - 1, 0))
-                residual = planes_of(f_vm.at[k], t) - x + planes_of(c_vm, t) * (beside - 6.0 * x)
-                for part, value in enumerate(halves(residual)):
-                    split_vm[part, at, tile(t % 4)] = value
+        for t in range(TILES):
+            x, turned = values[t], swapped[t]
+            beside = turned + jnp.where(low_half, swapped[t - 1], swapped[(t + 1) % TILES])
+            beside += pltpu.roll(jnp.where(last_col, turned, x), 1, 1)
+            beside += pltpu.roll(jnp.where(first_col, turned, x), LANES - 1, 1)
+            beside += jnp.where(row == 0, 0.0, pltpu.roll(x, 1, 0))
+            beside += jnp.where(row == PLANES - 1, 0.0, pltpu.roll(x, PLANES - 1, 0))
+            beside_vm[t] = beside - 6.0 * x
+        if k == 0:
+            c_copy.wait()
+            packed_planes(COMPS, c_vm)
+        f_copies[k].wait()
+        for t in range(TILES):
+            scaled = planes_of(c_vm, t) * beside_vm[t]
+            residual = planes_of(f_vm.at[k], t) - planes_of(v_ref.at[k], t) + scaled
+            first = PLANES * (BLOCKS * k + t // 4)
+            for part, value in enumerate(halves(residual)):
+                split_vm[part, first : first + PLANES, tile(t % 4)] = value
 
     matrix = w_ref[...]
     sums = jnp.dot(split_vm[0], matrix, preferred_element_type=F32)
@@ -163,7 +172,7 @@
             right_ref[4 + j, :, tile(k)] = (sources[6:] + half_odds[-1:])[j]
         packed_planes(k, v_ref.at[k])
 
-    copies[-1].wait()
+    cv_copy.wait()
     for j in range(3):
         left_ref[4 + j, :, tile(COMPS)] = cv_ref[pl.ds(j, 8, 8), :]
         right_ref[4 + j, :, tile(COMPS)] = cv_ref[pl.ds(min(6 + j, 7), 8, 8), :]
@@ -454,6 +463,7 @@
             pltpu.VMEM((COMPS,) + FINE_TILED, F32),
             pltpu.VMEM(FINE_TILED, F32),
             pltpu.VMEM((2, COMPS * BLOCKS * PLANES, WIDE), BF16),
+            pltpu.VMEM((TILES, PLANES, LANES), F32),
             pltpu.SemaphoreType.DMA((2 + 2 * COMPS,)),
         ],
         compiler_params=PARAMS,

time: 21.7 us -> 21.8 us (level)
  no operation moved by 1% of the time
where the time goes in v7:
time: 21.8 us; the launch traced here: 21.6 us
  starting transfers between devices  13.3 us (61%)
  Pallas kernels  5.63 us (26%)
  waiting for transfers between devices  1.99 us (9%)
  between operations  0.68 us (3%)
    ppermute x1, starting transfers between devices, shards(): outer_got = lax.ppermute(left_sent, axes, outer)  7.11 us
    ppermute x1, starting transfers between devices, shards(): lax.ppermute(right_sent, axes, [(i, i + 1) for i in range(count - 1)])  4.91 us
    pallas_call x1, Pallas kernels, shards(): pl.pallas_call(local_kernel, out_shape=(message, message, crosses, fine,...  2.49 us
    pallas_call x1, Pallas kernels, shards(): pl.pallas_call(lower_kernel, out_shape=(fine, coarse), in_specs=[HBM] + [...  1.55 us
    pallas_call x1, Pallas kernels, shards(): pl.pallas_call(upper_kernel, out_shape=(message, fine, jax.ShapeDtypeStru...  1.53 us
    ppermute x1, starting transfers between devices, shards(): inner_got = lax.ppermute(left_sent, axes, inner)  1.29 us
    ppermute x1, waiting for transfers between devices, shards(): inner_got = lax.ppermute(left_sent, axes, inner)  1.2 us
    ppermute x1, waiting for transfers between devices, shards(): lax.ppermute(right_sent, axes, [(i, i + 1) for i in range(count - 1)])  0.55 us
  transfers between devices with their start and end apart: 3, of which 3 were waited for; matrix products, arithmetic and copies ran while one was open for 0% of the time, Pallas kernels for 14%

profile of v7, /device:TPU:56, one launch (start us, length us, event | category | flops | bytes accessed | tf_op | source)
XLA Modules:
  0.0 21.6 jit_solution(806437944201893782)
XLA Ops:
  0.6 2.5 %shard_map.59 = (f32[7,8,512]{2,1,0:T(8,128)S(1)}, f32[7,8,512]{2,1,0:T(8,128)S(1)}, f32[3,128,128]{2,1,0:T(8,128)S(1)}, f32[3,2,256,128]{3,2,1,0:T(8,128)S(1)},...) custom-call(f32[3,2,256,128]{3,2,1,0:T(8,128)} %bitcast.31, ...), custom_call_target="tpu_custom_call" | custom-call | tf_op jit(solution)/shard_map/pallas_call | solution.py:449
  3.1 1.3 %collective-permute-start = (f32[7,8,512]{2,1,0:T(8,128)S(1)}, f32[7,8,512]{2,1,0:T(8,128)S(1)}, u32[]{:S(2)}, u32[]{:S(2)}) collective-permute-start(f32[7,8,512]{2,1,0:T(8,128)S(1)} %get-tuple-element.16.left_in), channel_id=1, source_target_pairs={{1,0},{2,1},{3,2},{4,3},{5,4},{6,5},{9,8},{10,9},{11,10},{12,11},{... | collective-permute-start | bytes 344072 | tf_op jit(solution)/shard_map/ppermute | solution.py:482
  4.4 4.9 %collective-permute-start.1 = (f32[7,8,512]{2,1,0:T(8,128)S(1)}, f32[7,8,512]{2,1,0:T(8,128)S(1)}, u32[]{:S(2)}, u32[]{:S(2)}) collective-permute-start(f32[7,8,512]{2,1,0:T(8,128)S(1)} %get-tuple-element.17.right_sent), channel_id=1, source_target_pairs={{0,1},{1,2},{2,3},{3,4},{4,5},{5,6},{6,7},{7,8},{8,9},{9,10},{10,1... | collective-permute-start | bytes 344072 | tf_op jit(solution)/shard_map/ppermute | solution.py:481
  9.3 1.2 %collective-permute-done.inner_got = f32[7,8,512]{2,1,0:T(8,128)S(1)} collective-permute-done((f32[7,8,512]{2,1,0:T(8,128)S(1)}, f32[7,8,512]{2,1,0:T(8,128)S(1)}, u32[]{:S(2)}, u32[]{:S(2)}) %collective-permute-start) | collective-permute-done | bytes 114720 | tf_op jit(solution)/shard_map/ppermute | solution.py:482
  10.5 1.5 %shard_map.60 = (f32[7,8,512]{2,1,0:T(8,128)S(1)}, f32[3,2,256,128]{3,2,1,0:T(8,128)}, f32[3,32,128]{2,1,0:T(8,128)S(1)}) custom-call(f32[7,8,512]{2,1,0:T(8,128)S(1)} %get-tuple-element.16.left_in, f32[7,8,512]{2,1,0:T(8,128)S(1)} %get-tuple-element.17.right_sent, f32[7,8,512]{2,1,0:T(8,128)S(1)} %collective-permute-done.inner_got, ...), custom_call_target="tpu_custom_call", output_to_operand_aliasing={{0}: (0, {})} | custom-call | tf_op jit(solution)/shard_map/pallas_call | solution.py:487
  12.1 7.1 %collective-permute-start.2 = (f32[7,8,512]{2,1,0:T(8,128)S(1)}, f32[7,8,512]{2,1,0:T(8,128)S(1)}, u32[]{:S(2)}, u32[]{:S(2)}) collective-permute-start(f32[7,8,512]{2,1,0:T(8,128)S(1)} %get-tuple-element.25.left_sent), channel_id=1, source_target_pairs={{7,6},{8,7},{15,14},{16,15},{23,22},{24,23},{31,30},{32,31},{39,38... | collective-permute-start | bytes 344072 | tf_op jit(solution)/shard_map/ppermute | solution.py:496
  19.2 0.5 %collective-permute-done.1.right_got = f32[7,8,512]{2,1,0:T(8,128)S(1)} collective-permute-done((f32[7,8,512]{2,1,0:T(8,128)S(1)}, f32[7,8,512]{2,1,0:T(8,128)S(1)}, u32[]{:S(2)}, u32[]{:S(2)}) %collective-permute-start.1) | collective-permute-done | bytes 114720 | tf_op jit(solution)/shard_map/ppermute | solution.py:481
  19.7 1.5 %shard_map.61 = (f32[3,2,256,128]{3,2,1,0:T(8,128)}, f32[3,64,128]{2,1,0:T(8,128)}) custom-call(f32[3,2,256,128]{3,2,1,0:T(8,128)} %get-tuple-element.23.out_in, f32[3,32,128]{2,1,0:T(8,128)S(1)} %get-tuple-element.24.upper_fix, f32[7,8,512]{2,1,0:T(8,128)S(1)} %get-tuple-element.25.left_sent, ...), custom_call_target="tpu_custom_call", output_to_operand_aliasing={{0}: (0, {})} | custom-call | tf_op jit(solution)/shard_map/pallas_call | solution.py:502
  21.3 0.2 %collective-permute-done.2.outer_got = f32[7,8,512]{2,1,0:T(8,128)S(1)} collective-permute-done((f32[7,8,512]{2,1,0:T(8,128)S(1)}, f32[7,8,512]{2,1,0:T(8,128)S(1)}, u32[]{:S(2)}, u32[]{:S(2)}) %collective-permute-start.2) | collective-permute-done | bytes 114720 | tf_op jit(solution)/shard_map/ppermute | solution.py:496
  21.5 0.1 shard_map.62
Async XLA Ops:
  3.1 7.4 %collective-permute-start = (f32[7,8,512]{2,1,0:T(8,128)S(1)}, f32[7,8,512]{2,1,0:T(8,128)S(1)}, u32[]{:S(2)}, u32[]{:S(2)}) collective-permute-start(f32[7,8,512]{2,1,0:T(8,128)S(1)} %get-tuple-element.16.left_in), channel_id=1, source_target_pairs={{1,0},{2,1},{3,2},{4,3},{5,4},{6,5},{9,8},{10,9},{11,10},{12,11},{... | collective-permute-start | bytes 344072 | tf_op jit(solution)/shard_map/ppermute | solution.py:482
  4.4 15.3 %collective-permute-start.1 = (f32[7,8,512]{2,1,0:T(8,128)S(1)}, f32[7,8,512]{2,1,0:T(8,128)S(1)}, u32[]{:S(2)}, u32[]{:S(2)}) collective-permute-start(f32[7,8,512]{2,1,0:T(8,128)S(1)} %get-tuple-element.17.right_sent), channel_id=1, source_target_pairs={{0,1},{1,2},{2,3},{3,4},{4,5},{5,6},{6,7},{7,8},{8,9},{9,10},{10,1... | collective-permute-start | bytes 344072 | tf_op jit(solution)/shard_map/ppermute | solution.py:481
  12.1 9.5 %collective-permute-start.2 = (f32[7,8,512]{2,1,0:T(8,128)S(1)}, f32[7,8,512]{2,1,0:T(8,128)S(1)}, u32[]{:S(2)}, u32[]{:S(2)}) collective-permute-start(f32[7,8,512]{2,1,0:T(8,128)S(1)} %get-tuple-element.25.left_sent), channel_id=1, source_target_pairs={{7,6},{8,7},{15,14},{16,15},{23,22},{24,23},{31,30},{32,31},{39,38... | collective-permute-start | bytes 344072 | tf_op jit(solution)/shard_map/ppermute | solution.py:496

commit v8 on v6

--- a/solution.py
+++ b/solution.py
@@ -121,6 +121,7 @@
     for k in range(COMPS):
         copies[1 + 2 * k].wait()
         copies[2 + 2 * k].wait()
+        packed_planes(k, v_ref.at[k])
 
         def planes_of(ref, t):
             return jnp.concatenate([ref[0, eight(t), :], ref[1, eight(t), :]], axis=0)
@@ -161,7 +162,6 @@
         for j in range(3):
             left_ref[4 + j, :, tile(k)] = sources[j]
             right_ref[4 + j, :, tile(k)] = (sources[6:] + half_odds[-1:])[j]
-        packed_planes(k, v_ref.at[k])
 
     copies[-1].wait()
     for j in range(3):
@@ -208,8 +208,8 @@
         total = planes[j - 1] + planes[j + 1]
         total += jnp.where(kept_up, up, pltpu.roll(up, 7, 0))
         total += jnp.where(kept_down, down, pltpu.roll(down, 1, 0))
-        total += pltpu.roll(jnp.where(last_col, up, x), 1, 1)
-        total += pltpu.roll(jnp.where(first_col, down, x), LANES - 1, 1)
+        total += jnp.where(first_col, pltpu.roll(x, LANES - NZ + 1, 1), pltpu.roll(x, 1, 1))
+        total += jnp.where(last_col, pltpu.roll(x, NZ - 1, 1), pltpu.roll(x, LANES - 1, 1))
         return total
 
     sigma = CENTER / HALF_WIDTH

time: 21.7 us -> 21.7 us (level)
  Pallas kernels: 5.58 us -> 5.26 us
  transfers between devices with their start and end apart: 3 -> 3, of which waited for: 3 -> 3; matrix products, arithmetic and copies ran while one was open for 0% -> 0% of each run, Pallas kernels for 14% -> 13%
where the time goes in v8:
time: 21.7 us; the launch traced here: 21.5 us
  starting transfers between devices  13.5 us (62%)
  Pallas kernels  5.26 us (24%)
  waiting for transfers between devices  2.16 us (10%)
  between operations  0.68 us (3%)
    ppermute x1, starting transfers between devices, shards(): outer_got = lax.ppermute(left_sent, axes, outer)  7.26 us
    ppermute x1, starting transfers between devices, shards(): lax.ppermute(right_sent, axes, [(i, i + 1) for i in range(count - 1)])  4.9 us
    pallas_call x1, Pallas kernels, shards(): pl.pallas_call(local_kernel, out_shape=(message, message, crosses, fine,...  2.44 us
    pallas_call x1, Pallas kernels, shards(): pl.pallas_call(lower_kernel, out_shape=(fine, coarse), in_specs=[HBM] + [...  1.38 us
    pallas_call x1, Pallas kernels, shards(): pl.pallas_call(upper_kernel, out_shape=(message, fine, jax.ShapeDtypeStru...  1.37 us
    ppermute x1, starting transfers between devices, shards(): inner_got = lax.ppermute(left_sent, axes, inner)  1.29 us
    ppermute x1, waiting for transfers between devices, shards(): inner_got = lax.ppermute(left_sent, axes, inner)  1.21 us
    ppermute x1, waiting for transfers between devices, shards(): lax.ppermute(right_sent, axes, [(i, i + 1) for i in range(count - 1)])  0.55 us
  transfers between devices with their start and end apart: 3, of which 3 were waited for; matrix products, arithmetic and copies ran while one was open for 0% of the time, Pallas kernels for 13%

profile of v8, /device:TPU:56, one launch (start us, length us, event | category | flops | bytes accessed | tf_op | source)
XLA Modules:
  0.0 21.5 jit_solution(9171191915570475233)
XLA Ops:
  0.6 2.4 %shard_map.59 = (f32[7,8,512]{2,1,0:T(8,128)S(1)}, f32[7,8,512]{2,1,0:T(8,128)S(1)}, f32[3,128,128]{2,1,0:T(8,128)S(1)}, f32[3,2,256,128]{3,2,1,0:T(8,128)S(1)},...) custom-call(f32[3,2,256,128]{3,2,1,0:T(8,128)} %bitcast.31, ...), custom_call_target="tpu_custom_call" | custom-call | tf_op jit(solution)/shard_map/pallas_call | solution.py:440
  3.1 1.3 %collective-permute-start = (f32[7,8,512]{2,1,0:T(8,128)S(1)}, f32[7,8,512]{2,1,0:T(8,128)S(1)}, u32[]{:S(2)}, u32[]{:S(2)}) collective-permute-start(f32[7,8,512]{2,1,0:T(8,128)S(1)} %get-tuple-element.16.left_in), channel_id=1, source_target_pairs={{1,0},{2,1},{3,2},{4,3},{5,4},{6,5},{9,8},{10,9},{11,10},{12,11},{... | collective-permute-start | bytes 344072 | tf_op jit(solution)/shard_map/ppermute | solution.py:472
  4.4 4.9 %collective-permute-start.1 = (f32[7,8,512]{2,1,0:T(8,128)S(1)}, f32[7,8,512]{2,1,0:T(8,128)S(1)}, u32[]{:S(2)}, u32[]{:S(2)}) collective-permute-start(f32[7,8,512]{2,1,0:T(8,128)S(1)} %get-tuple-element.17.right_sent), channel_id=1, source_target_pairs={{0,1},{1,2},{2,3},{3,4},{4,5},{5,6},{6,7},{7,8},{8,9},{9,10},{10,1... | collective-permute-start | bytes 344072 | tf_op jit(solution)/shard_map/ppermute | solution.py:471
  9.3 1.2 %collective-permute-done.inner_got = f32[7,8,512]{2,1,0:T(8,128)S(1)} collective-permute-done((f32[7,8,512]{2,1,0:T(8,128)S(1)}, f32[7,8,512]{2,1,0:T(8,128)S(1)}, u32[]{:S(2)}, u32[]{:S(2)}) %collective-permute-start) | collective-permute-done | bytes 114720 | tf_op jit(solution)/shard_map/ppermute | solution.py:472
  10.5 1.4 %shard_map.60 = (f32[7,8,512]{2,1,0:T(8,128)S(1)}, f32[3,2,256,128]{3,2,1,0:T(8,128)}, f32[3,32,128]{2,1,0:T(8,128)S(1)}) custom-call(f32[7,8,512]{2,1,0:T(8,128)S(1)} %get-tuple-element.16.left_in, f32[7,8,512]{2,1,0:T(8,128)S(1)} %get-tuple-element.17.right_sent, f32[7,8,512]{2,1,0:T(8,128)S(1)} %collective-permute-done.inner_got, ...), custom_call_target="tpu_custom_call", output_to_operand_aliasing={{0}: (0, {})} | custom-call | tf_op jit(solution)/shard_map/pallas_call | solution.py:477
  11.9 7.3 %collective-permute-start.2 = (f32[7,8,512]{2,1,0:T(8,128)S(1)}, f32[7,8,512]{2,1,0:T(8,128)S(1)}, u32[]{:S(2)}, u32[]{:S(2)}) collective-permute-start(f32[7,8,512]{2,1,0:T(8,128)S(1)} %get-tuple-element.25.left_sent), channel_id=1, source_target_pairs={{7,6},{8,7},{15,14},{16,15},{23,22},{24,23},{31,30},{32,31},{39,38... | collective-permute-start | bytes 344072 | tf_op jit(solution)/shard_map/ppermute | solution.py:486
  19.1 0.5 %collective-permute-done.1.right_got = f32[7,8,512]{2,1,0:T(8,128)S(1)} collective-permute-done((f32[7,8,512]{2,1,0:T(8,128)S(1)}, f32[7,8,512]{2,1,0:T(8,128)S(1)}, u32[]{:S(2)}, u32[]{:S(2)}) %collective-permute-start.1) | collective-permute-done | bytes 114720 | tf_op jit(solution)/shard_map/ppermute | solution.py:471
  19.7 1.4 %shard_map.61 = (f32[3,2,256,128]{3,2,1,0:T(8,128)}, f32[3,64,128]{2,1,0:T(8,128)}) custom-call(f32[3,2,256,128]{3,2,1,0:T(8,128)} %get-tuple-element.23.out_in, f32[3,32,128]{2,1,0:T(8,128)S(1)} %get-tuple-element.24.upper_fix, f32[7,8,512]{2,1,0:T(8,128)S(1)} %get-tuple-element.25.left_sent, ...), custom_call_target="tpu_custom_call", output_to_operand_aliasing={{0}: (0, {})} | custom-call | tf_op jit(solution)/shard_map/pallas_call | solution.py:492
  21.1 0.4 %collective-permute-done.2.outer_got = f32[7,8,512]{2,1,0:T(8,128)S(1)} collective-permute-done((f32[7,8,512]{2,1,0:T(8,128)S(1)}, f32[7,8,512]{2,1,0:T(8,128)S(1)}, u32[]{:S(2)}, u32[]{:S(2)}) %collective-permute-start.2) | collective-permute-done | bytes 114720 | tf_op jit(solution)/shard_map/ppermute | solution.py:486
  21.5 0.1 shard_map.62
Async XLA Ops:
  3.1 7.4 %collective-permute-start = (f32[7,8,512]{2,1,0:T(8,128)S(1)}, f32[7,8,512]{2,1,0:T(8,128)S(1)}, u32[]{:S(2)}, u32[]{:S(2)}) collective-permute-start(f32[7,8,512]{2,1,0:T(8,128)S(1)} %get-tuple-element.16.left_in), channel_id=1, source_target_pairs={{1,0},{2,1},{3,2},{4,3},{5,4},{6,5},{9,8},{10,9},{11,10},{12,11},{... | collective-permute-start | bytes 344072 | tf_op jit(solution)/shard_map/ppermute | solution.py:472
  4.4 15.3 %collective-permute-start.1 = (f32[7,8,512]{2,1,0:T(8,128)S(1)}, f32[7,8,512]{2,1,0:T(8,128)S(1)}, u32[]{:S(2)}, u32[]{:S(2)}) collective-permute-start(f32[7,8,512]{2,1,0:T(8,128)S(1)} %get-tuple-element.17.right_sent), channel_id=1, source_target_pairs={{0,1},{1,2},{2,3},{3,4},{4,5},{5,6},{6,7},{7,8},{8,9},{9,10},{10,1... | collective-permute-start | bytes 344072 | tf_op jit(solution)/shard_map/ppermute | solution.py:471
  11.9 9.6 %collective-permute-start.2 = (f32[7,8,512]{2,1,0:T(8,128)S(1)}, f32[7,8,512]{2,1,0:T(8,128)S(1)}, u32[]{:S(2)}, u32[]{:S(2)}) collective-permute-start(f32[7,8,512]{2,1,0:T(8,128)S(1)} %get-tuple-element.25.left_sent), channel_id=1, source_target_pairs={{7,6},{8,7},{15,14},{16,15},{23,22},{24,23},{31,30},{32,31},{39,38... | collective-permute-start | bytes 344072 | tf_op jit(solution)/shard_map/ppermute | solution.py:486
